TPU v7x, 128 devices: a whole 4x4x4 slice. The times are simulated.
128 devices in a mesh: dp: 2 (over z_lo), ty: 8 (over x, core), tz: 8 (over y, z_hi).
Axes of the slice: x: 4, y: 4, z: 4 (z_hi: 2, z_lo: 2; z = z_hi * 2 + z_lo), core: 2. Of those that a mesh axis runs over, the one named last changes fastest.
Arguments:
- fine_input: bfloat16 [2, 16, 2, 512, 1024], P('dp', None, None, 'ty', 'tz'), may hold values from -6 to 6
- fine_cotangent: bfloat16 [2, 16, 2, 512, 1024], P('dp', None, None, 'ty', 'tz'), may hold values from -6 to 6
- first_weight: bfloat16 [27, 16, 16], replicated, may hold values from -0.3125 to 0.3125
- second_weight: bfloat16 [27, 16, 16], replicated, may hold values from -0.3125 to 0.3125
- coarse_input: bfloat16 [2, 16, 64, 64, 128], P('dp', None, 'ty', 'tz'), may hold values from -6 to 6
- coarse_cotangent: bfloat16 [2, 16, 64, 64, 128], P('dp', None, 'ty', 'tz'), may hold values from -6 to 6
- coarse_weight: bfloat16 [27, 128, 128], replicated, may hold values from -0.109375 to 0.109375
Outputs:
- grad_fine_input: bfloat16 [2, 16, 2, 512, 1024], P('dp', None, None, 'ty', 'tz')
- grad_first: float32 [27, 16, 16], replicated
- grad_second: float32 [27, 16, 16], replicated
- grad_coarse_input: bfloat16 [2, 16, 64, 64, 128], P('dp', None, 'ty', 'tz')
- grad_coarse: float32 [128, 27, 128], P(('ty', 'tz'))
All inputs are finite; a program needn't handle non-finite values.
Results may differ from a plain program's by a relative error of at most 0.0049.
Values may be sent and summed in bfloat16 or wider, within the bound.
A program may use at most 320 MiB of HBM per device.

v0:
```python
import jax
import jax.numpy as jnp
from jax import lax
from jax.sharding import PartitionSpec as P


def with_halo(cells, sides, width):
    for axis, dim in sides:
        count = lax.axis_size(axis)
        ends = count - 1
        head = lax.slice_in_dim(cells, 0, width, axis=dim)
        tail = lax.slice_in_dim(cells, cells.shape[dim] - width, cells.shape[dim], axis=dim)
        cells = jnp.concatenate(
            [
                lax.ppermute(tail, axis, [(i, (i + 1) % count) for i in range(ends)]),
                cells,
                lax.ppermute(head, axis, [((i + 1) % count, i) for i in range(ends)]),
            ],
            axis=dim,
        )
    return cells


def offsets():
    return [(kk // 9, kk // 3 % 3, kk % 3) for kk in range(27)]


def pad_planes(values):
    return jnp.pad(values, ((0, 0), (0, 0), (1, 1), (0, 0), (0, 0)))


def forward_conv(source, weight):
    depth, height, width = (source.shape[2] - 2, source.shape[3] - 2, source.shape[4] - 2)
    summed = None
    for sx, sy, sz in offsets():
        window = source[:, :, sx : sx + depth, sy : sy + height, sz : sz + width]
        contrib = jnp.einsum(
            "oc,bcxyz->boxyz",
            weight[9 * sx + 3 * sy + sz],
            window,
            preferred_element_type=jnp.float32,
        )
        summed = contrib if summed is None else summed + contrib
    return summed


def transposed_conv(source, weight):
    depth, height, width = (source.shape[2] - 2, source.shape[3] - 2, source.shape[4] - 2)
    summed = None
    for sx, sy, sz in offsets():
        window = source[
            :, :, 2 - sx : 2 - sx + depth, 2 - sy : 2 - sy + height, 2 - sz : 2 - sz + width
        ]
        contrib = jnp.einsum(
            "oc,boxyz->bcxyz",
            weight[9 * sx + 3 * sy + sz],
            window,
            preferred_element_type=jnp.float32,
        )
        summed = contrib if summed is None else summed + contrib
    return summed


def weight_grad(cotangent, source):
    depth, height, width = (cotangent.shape[2], cotangent.shape[3], cotangent.shape[4])
    parts = []
    for sx, sy, sz in offsets():
        window = source[:, :, sx : sx + depth, sy : sy + height, sz : sz + width]
        parts.append(
            jnp.einsum("boxyz,bcxyz->oc", cotangent, window, preferred_element_type=jnp.float32)
        )
    return jnp.stack(parts, 0)


def transposed_last(source, weight):
    depth, height, width = (source.shape[1] - 2, source.shape[2] - 2, source.shape[3] - 2)
    summed = None
    for sx, sy, sz in offsets():
        window = source[
            :, 2 - sx : 2 - sx + depth, 2 - sy : 2 - sy + height, 2 - sz : 2 - sz + width
        ]
        contrib = jnp.einsum(
            "bxyzo,oc->bxyzc",
            window,
            weight[9 * sx + 3 * sy + sz],
            preferred_element_type=jnp.float32,
        )
        summed = contrib if summed is None else summed + contrib
    return summed


def weight_grad_last(cotangent, source):
    depth, height, width = (cotangent.shape[1], cotangent.shape[2], cotangent.shape[3])
    parts = []
    for sx, sy, sz in offsets():
        window = source[:, sx : sx + depth, sy : sy + height, sz : sz + width]
        parts.append(
            jnp.einsum("bxyzo,bxyzc->oc", cotangent, window, preferred_element_type=jnp.float32)
        )
    return jnp.stack(parts, 1)


def gelu_back(pre, dact):
    return jax.vjp(jax.nn.gelu, pre)[1](dact)[0]


def per_device(
    fine_input,
    fine_cotangent,
    first_weight,
    second_weight,
    coarse_input,
    coarse_cotangent,
    coarse_weight,
):
    channels = fine_input.shape[1]
    wide = coarse_input.shape[4]
    joined = jnp.concatenate([coarse_input, coarse_cotangent], 4)
    rimmed = with_halo(joined, (("ty", 2), ("tz", 3)), 1)
    rimmed = jnp.pad(rimmed, ((0, 0), (1, 1), (0, 0), (0, 0), (0, 0)))
    grad_coarse_input = transposed_last(rimmed[..., wide:], coarse_weight).astype(jnp.bfloat16)
    coarse_terms = weight_grad_last(coarse_cotangent, rimmed[..., :wide])
    stacked = jnp.concatenate([fine_input, fine_cotangent], 1)
    outer = with_halo(stacked, (("ty", 3), ("tz", 4)), 1)
    source_rim = outer[:, :channels]
    pre = forward_conv(pad_planes(source_rim), first_weight)
    act = jax.nn.gelu(pre).astype(jnp.bfloat16)
    dact = transposed_conv(pad_planes(outer[:, channels:]), second_weight)
    dpre = gelu_back(pre, dact).astype(jnp.bfloat16)
    inner = with_halo(jnp.concatenate([act, dpre], 1), (("ty", 3), ("tz", 4)), 1)
    second_terms = weight_grad(fine_cotangent, pad_planes(inner[:, :channels]))
    first_terms = weight_grad(dpre, pad_planes(source_rim))
    grad_fine_input = transposed_conv(pad_planes(inner[:, channels:]), first_weight).astype(
        jnp.bfloat16
    )
    grad_first, grad_second, coarse_all = lax.psum(
        (first_terms, second_terms, coarse_terms), ("dp", "ty", "tz")
    )
    owners = lax.axis_size("ty") * lax.axis_size("tz")
    rows = coarse_all.shape[0] // owners
    start = (lax.axis_index("ty") * lax.axis_size("tz") + lax.axis_index("tz")) * rows
    grad_coarse = lax.dynamic_slice_in_dim(coarse_all, start, rows, 0)
    return (grad_fine_input, grad_first, grad_second, grad_coarse_input, grad_coarse)


def solution(mesh):
    in_specs = (
        P("dp", None, None, "ty", "tz"),
        P("dp", None, None, "ty", "tz"),
        P(),
        P(),
        P("dp", None, "ty", "tz", None),
        P("dp", None, "ty", "tz", None),
        P(),
    )
    out_specs = (
        P("dp", None, None, "ty", "tz"),
        P(),
        P(),
        P("dp", None, "ty", "tz", None),
        P(("ty", "tz"), None, None),
    )
    return jax.shard_map(
        per_device, mesh=mesh, in_specs=in_specs, out_specs=out_specs, check_vma=False
    )
```

profile of v0, /device:TPU:1, one launch (start us, length us, event | category | flops | bytes accessed | tf_op | source)
XLA Modules:
  0.0 575.7 jit_solution(366432613710253996)
XLA Ops:
  10.0 4.5 collective-permute-start.8
  18.8 3.6 collective-permute-start
  22.4 2.1 collective-permute-start.1
  103.6 3.2 copy.186
  106.8 6.1 %collective-permute-start.2 = (bf16[1,32,2,66,1]{3,1,4,2,0:T(8,128)(2,1)}, bf16[1,32,2,66,1]{3,1,4,2,0:T(8,128)(2,1)}, u32[]{:S(2)}, u32[]{:S(2)}) collective-permute-start(bf16[1,32,2,66,1]{3,1,4,2,0:T(8,128)(2,1)} %copy.186), channel_id=1, source_target_pairs={{0,1},{1,2},{2,3},{3,4},{4,5},{5,6},{6,7},{8,9},{9,10},{10,11},{11... | collective-permute-start | bytes 25352 | tf_op jit(solution)/shard_map/ppermute | solution.py:15
  122.2 2.5 copy.188
  124.7 3.4 copy.189
  128.1 3.0 pad_maximum_fusion
  132.3 2.1 pad_maximum_fusion.1
  156.4 12.3 %fusion.20 = f32[2,64,128,16]{2,3,1,0:T(8,128)S(1)} fusion(f32[2,64,128,16]{2,3,1,0:T(8,128)S(1)} %copy-done.6, f32[2,64,128,16]{2,3,1,0:T(8,128)S(1)} %fusion.362, f32[2,64,128,16]{2,3,1,0:T(8,128)S(1)} %fusion.361, f32[2,64,128,16]{2,3,1,0:T(8,128)S(1)} %copy-done.12, f32[2,64,128,16]{2,3,1,0:T(8,128)S(1)} %convolution_add_fusion.12, ...), kind=kOutput, calls=%fused_computation.167 | convolution fusion | flops 9699328 | bytes 6819840 | tf_op jit(solution)/shard_map/oc,bcxyz->boxyz/dot_general | solution.py:37
  173.5 3.9 collective-permute-start.4
  192.1 2.4 copy.248
  194.5 5.9 %collective-permute-start.6 = (bf16[1,32,2,66,1]{3,1,4,2,0:T(8,128)(2,1)S(1)}, bf16[1,32,2,66,1]{3,1,4,2,0:T(8,128)(2,1)S(1)}, u32[]{:S(2)}, u32[]{:S(2)}) collective-permute-start(bf16[1,32,2,66,1]{3,1,4,2,0:T(8,128)(2,1)S(1)} %copy.248), channel_id=1, source_target_pairs={{0,1},{1,2},{2,3},{3,4},{4,5},{5,6},{6,7},{8,9},{9,10},{10,11},{11... | collective-permute-start | bytes 25352 | tf_op jit(solution)/shard_map/ppermute | solution.py:15
  200.4 2.4 copy.249
  206.8 2.7 copy.250
  209.5 2.7 copy.251
  212.2 3.7 maximum_maximum_fusion.1
  217.5 2.6 pad_maximum_fusion.2
  260.9 72.4 %all-reduce.5 = (f32[27,16,16]{2,1,0:T(8,128)S(1)}, f32[27,16,16]{1,2,0:T(8,128)S(1)}) all-reduce(f32[27,16,16]{2,1,0:T(8,128)S(1)} %copy-done.43, f32[27,16,16]{1,2,0:T(8,128)} %fusion.114), channel_id=1, replica_groups=mesh['dp'=2,'ty'=8,'tz'=8] {'dp','ty','tz'}, use_global_device_ids=true, to_apply=%region_0.1 | all-reduce | flops 13824 | bytes 110592 | tf_op jit(solution)/shard_map/psum | solution.py:136
  337.0 3.8 collective-permute-start.10
  345.7 4.4 collective-permute-done.11
  418.0 3.5 fusion.72
  424.5 141.0 %all-reduce.8.cloned.1.call-done = f32[128,27,128]{0,2,1:T(8,128)} async-done(((f32[128,27,128]{0,2,1:T(8,128)}), f32[128,27,128]{0,2,1:T(8,128)}) %all-reduce.8.cloned.1.call-update) | async-done | bytes 1769488 | tf_op jit(solution)/shard_map/psum | solution.py:136
  565.5 2.0 constant_dynamic-slice_fusion
  (514 shorter events, 263.8 us)
Async XLA Ops:
  7.2 558.3 %all-reduce.8.cloned.1.call-start = ((), (), s32[]{:S(2)}) async-start(), calls=%async_computation | async-start | bytes 3538944 | tf_op jit(solution)/shard_map/psum | solution.py:136
  10.0 325.9 %collective-permute-start.8 = (bf16[1,16,1,8,256]{4,3,2,1,0:T(8,128)(2,1)}, bf16[1,16,1,8,256]{4,3,2,1,0:T(8,128)(2,1)}, u32[]{:S(2)}, u32[]{:S(2)}) collective-permute-start(bf16[1,16,1,8,256]{4,3,2,1,0:T(8,128)(2,1)} %get-tuple-element.37), channel_id=1, source_target_pairs={{0,8},{8,16},{16,24},{24,32},{32,40},{40,48},{48,56},{1,9},{9,17},... | collective-permute-start | bytes 196616 | tf_op jit(solution)/shard_map/ppermute | solution.py:15
  14.5 321.4 %collective-permute-start.9 = (bf16[1,16,1,8,256]{4,3,2,1,0:T(8,128)(2,1)}, bf16[1,16,1,8,256]{4,3,2,1,0:T(8,128)(2,1)S(1)}, u32[]{:S(2)}, u32[]{:S(2)}) collective-permute-start(bf16[1,16,1,8,256]{4,3,2,1,0:T(8,128)(2,1)} %get-tuple-element.38), channel_id=1, source_target_pairs={{8,0},{16,8},{24,16},{32,24},{40,32},{48,40},{56,48},{9,1},{17,9},... | collective-permute-start | bytes 196616 | tf_op jit(solution)/shard_map/ppermute | solution.py:17
  18.8 83.2 %collective-permute-start = (bf16[1,32,2,1,128]{4,1,3,2,0:T(8,128)(2,1)}, bf16[1,32,2,1,128]{4,1,3,2,0:T(8,128)(2,1)S(1)}, u32[]{:S(2)}, u32[]{:S(2)}) collective-permute-start(bf16[1,32,2,1,128]{4,1,3,2,0:T(8,128)(2,1)} %get-tuple-element.31), channel_id=1, source_target_pairs={{0,8},{8,16},{16,24},{24,32},{32,40},{40,48},{48,56},{1,9},{9,17},... | collective-permute-start | bytes 49160 | tf_op jit(solution)/shard_map/ppermute | solution.py:15
  22.4 79.5 %collective-permute-start.1 = (bf16[1,32,2,1,128]{4,1,3,2,0:T(8,128)(2,1)S(1)}, bf16[1,32,2,1,128]{4,1,3,2,0:T(8,128)(2,1)S(1)}, u32[]{:S(2)}, u32[]{:S(2)}) collective-permute-start(bf16[1,32,2,1,128]{4,1,3,2,0:T(8,128)(2,1)S(1)} %get-tuple-element.32), channel_id=1, source_target_pairs={{8,0},{16,8},{24,16},{32,24},{40,32},{48,40},{56,48},{9,1},{17,9},... | collective-permute-start | bytes 49160 | tf_op jit(solution)/shard_map/ppermute | solution.py:17
  33.1 54.8 %copy-start.41 = (bf16[1,16,16]{0,2,1:T(8,128)(2,1)S(1)}, bf16[1,16,16]{0,2,1:T(8,128)(2,1)}, u32[]{:S(2)}) copy-start(bf16[1,16,16]{0,2,1:T(8,128)(2,1)} %get-tuple-element.70) | copy-start | bytes 1540
  33.1 55.6 %copy-start.40 = (bf16[1,16,16]{0,2,1:T(8,128)(2,1)S(1)}, bf16[1,16,16]{0,2,1:T(8,128)(2,1)}, u32[]{:S(2)}) copy-start(bf16[1,16,16]{0,2,1:T(8,128)(2,1)} %get-tuple-element.71) | copy-start | bytes 1540
  33.1 56.4 %copy-start.39 = (bf16[1,16,16]{0,2,1:T(8,128)(2,1)S(1)}, bf16[1,16,16]{0,2,1:T(8,128)(2,1)}, u32[]{:S(2)}) copy-start(bf16[1,16,16]{0,2,1:T(8,128)(2,1)} %get-tuple-element.72) | copy-start | bytes 1540
  33.1 57.1 %copy-start.38 = (bf16[1,16,16]{0,2,1:T(8,128)(2,1)S(1)}, bf16[1,16,16]{0,2,1:T(8,128)(2,1)}, u32[]{:S(2)}) copy-start(bf16[1,16,16]{0,2,1:T(8,128)(2,1)} %get-tuple-element.73) | copy-start | bytes 1540
  33.1 57.9 %copy-start.37 = (bf16[1,16,16]{0,2,1:T(8,128)(2,1)S(1)}, bf16[1,16,16]{0,2,1:T(8,128)(2,1)}, u32[]{:S(2)}) copy-start(bf16[1,16,16]{0,2,1:T(8,128)(2,1)} %get-tuple-element.74) | copy-start | bytes 1540
  33.1 60.3 %copy-start.36 = (bf16[1,16,16]{0,2,1:T(8,128)(2,1)S(1)}, bf16[1,16,16]{0,2,1:T(8,128)(2,1)}, u32[]{:S(2)}) copy-start(bf16[1,16,16]{0,2,1:T(8,128)(2,1)} %get-tuple-element.66) | copy-start | bytes 1540
  34.1 60.1 %copy-start.35 = (bf16[1,16,16]{0,2,1:T(8,128)(2,1)S(1)}, bf16[1,16,16]{0,2,1:T(8,128)(2,1)}, u32[]{:S(2)}) copy-start(bf16[1,16,16]{0,2,1:T(8,128)(2,1)} %get-tuple-element.40) | copy-start | bytes 1540
  34.1 60.8 %copy-start.34 = (bf16[1,16,16]{0,2,1:T(8,128)(2,1)S(1)}, bf16[1,16,16]{0,2,1:T(8,128)(2,1)}, u32[]{:S(2)}) copy-start(bf16[1,16,16]{0,2,1:T(8,128)(2,1)} %get-tuple-element.41) | copy-start | bytes 1540
  34.1 61.6 %copy-start.33 = (bf16[1,16,16]{0,2,1:T(8,128)(2,1)S(1)}, bf16[1,16,16]{0,2,1:T(8,128)(2,1)}, u32[]{:S(2)}) copy-start(bf16[1,16,16]{0,2,1:T(8,128)(2,1)} %get-tuple-element.42) | copy-start | bytes 1540
  34.1 62.4 %copy-start.32 = (bf16[1,16,16]{0,2,1:T(8,128)(2,1)S(1)}, bf16[1,16,16]{0,2,1:T(8,128)(2,1)}, u32[]{:S(2)}) copy-start(bf16[1,16,16]{0,2,1:T(8,128)(2,1)} %get-tuple-element.43) | copy-start | bytes 1540
  106.8 15.4 %collective-permute-start.2 = (bf16[1,32,2,66,1]{3,1,4,2,0:T(8,128)(2,1)}, bf16[1,32,2,66,1]{3,1,4,2,0:T(8,128)(2,1)}, u32[]{:S(2)}, u32[]{:S(2)}) collective-permute-start(bf16[1,32,2,66,1]{3,1,4,2,0:T(8,128)(2,1)} %copy.186), channel_id=1, source_target_pairs={{0,1},{1,2},{2,3},{3,4},{4,5},{5,6},{6,7},{8,9},{9,10},{10,11},{11... | collective-permute-start | bytes 25352 | tf_op jit(solution)/shard_map/ppermute | solution.py:15
  114.8 9.9 %collective-permute-start.3 = (bf16[1,32,2,66,1]{3,1,4,2,0:T(8,128)(2,1)}, bf16[1,32,2,66,1]{3,1,4,2,0:T(8,128)(2,1)}, u32[]{:S(2)}, u32[]{:S(2)}) collective-permute-start(bf16[1,32,2,66,1]{3,1,4,2,0:T(8,128)(2,1)} %copy.187), channel_id=1, source_target_pairs={{1,0},{2,1},{3,2},{4,3},{5,4},{6,5},{7,6},{9,8},{10,9},{11,10},{12... | collective-permute-start | bytes 25352 | tf_op jit(solution)/shard_map/ppermute | solution.py:17
  173.5 15.9 %collective-permute-start.4 = (bf16[1,32,2,1,128]{4,1,3,2,0:T(8,128)(2,1)S(1)}, bf16[1,32,2,1,128]{4,1,3,2,0:T(8,128)(2,1)S(1)}, u32[]{:S(2)}, u32[]{:S(2)}) collective-permute-start(bf16[1,32,2,1,128]{4,1,3,2,0:T(8,128)(2,1)S(1)} %get-tuple-element.29), channel_id=1, source_target_pairs={{0,8},{8,16},{16,24},{24,32},{32,40},{40,48},{48,56},{1,9},{9,17},... | collective-permute-start | bytes 49160 | tf_op jit(solution)/shard_map/ppermute | solution.py:15
  177.4 12.7 %collective-permute-start.5 = (bf16[1,32,2,1,128]{4,1,3,2,0:T(8,128)(2,1)S(1)}, bf16[1,32,2,1,128]{4,1,3,2,0:T(8,128)(2,1)S(1)}, u32[]{:S(2)}, u32[]{:S(2)}) collective-permute-start(bf16[1,32,2,1,128]{4,1,3,2,0:T(8,128)(2,1)S(1)} %get-tuple-element.30), channel_id=1, source_target_pairs={{8,0},{16,8},{24,16},{32,24},{40,32},{48,40},{56,48},{9,1},{17,9},... | collective-permute-start | bytes 49160 | tf_op jit(solution)/shard_map/ppermute | solution.py:17
  194.5 12.2 %collective-permute-start.6 = (bf16[1,32,2,66,1]{3,1,4,2,0:T(8,128)(2,1)S(1)}, bf16[1,32,2,66,1]{3,1,4,2,0:T(8,128)(2,1)S(1)}, u32[]{:S(2)}, u32[]{:S(2)}) collective-permute-start(bf16[1,32,2,66,1]{3,1,4,2,0:T(8,128)(2,1)S(1)} %copy.248), channel_id=1, source_target_pairs={{0,1},{1,2},{2,3},{3,4},{4,5},{5,6},{6,7},{8,9},{9,10},{10,11},{11... | collective-permute-start | bytes 25352 | tf_op jit(solution)/shard_map/ppermute | solution.py:15
  202.8 6.7 %collective-permute-start.7 = (bf16[1,32,2,66,1]{3,1,4,2,0:T(8,128)(2,1)S(1)}, bf16[1,32,2,66,1]{3,1,4,2,0:T(8,128)(2,1)S(1)}, u32[]{:S(2)}, u32[]{:S(2)}) collective-permute-start(bf16[1,32,2,66,1]{3,1,4,2,0:T(8,128)(2,1)S(1)} %copy.249), channel_id=1, source_target_pairs={{1,0},{2,1},{3,2},{4,3},{5,4},{6,5},{7,6},{9,8},{10,9},{11,10},{12... | collective-permute-start | bytes 25352 | tf_op jit(solution)/shard_map/ppermute | solution.py:17
  337.0 8.7 %collective-permute-start.10 = (bf16[1,16,10,1,256]{4,3,2,1,0:T(2,128)(2,1)S(1)}, bf16[1,16,10,1,256]{4,3,2,1,0:T(2,128)(2,1)S(1)}, u32[]{:S(2)}, u32[]{:S(2)}) collective-permute-start(bf16[1,16,10,1,256]{4,3,2,1,0:T(2,128)(2,1)S(1)} %get-tuple-element.35), channel_id=1, source_target_pairs={{0,1},{1,2},{2,3},{3,4},{4,5},{5,6},{6,7},{8,9},{9,10},{10,11},{11... | collective-permute-start | bytes 245768 | tf_op jit(solution)/shard_map/ppermute | solution.py:15
  340.8 9.3 %collective-permute-start.11 = (bf16[1,16,10,1,256]{4,3,2,1,0:T(2,128)(2,1)S(1)}, bf16[1,16,10,1,256]{4,3,2,1,0:T(2,128)(2,1)S(1)}, u32[]{:S(2)}, u32[]{:S(2)}) collective-permute-start(bf16[1,16,10,1,256]{4,3,2,1,0:T(2,128)(2,1)S(1)} %get-tuple-element.36), channel_id=1, source_target_pairs={{1,0},{2,1},{3,2},{4,3},{5,4},{6,5},{7,6},{9,8},{10,9},{11,10},{12... | collective-permute-start | bytes 245768 | tf_op jit(solution)/shard_map/ppermute | solution.py:17
  368.8 38.7 %copy-start.15 = (bf16[1,16,10,9,256]{4,3,2,1,0:T(8,128)(2,1)}, bf16[1,16,10,9,256]{4,3,2,1,0:T(8,128)(2,1)S(1)}, u32[]{:S(2)}) copy-start(bf16[1,16,10,9,256]{4,3,2,1,0:T(8,128)(2,1)S(1)} %get-tuple-element.33) | copy-start | bytes 2211844
  (104 other events, 232.9 us)
Sparse Core Ops, SparseCore 0:
  416.7 148.6 all-reduce.7
where the time goes:
time: 583 us; the launch traced here: 576 us
  matrix products  164 us (28%)
  waiting for transfers between devices  145 us (25%)
  local copies, waits for them, and re-layouts  124 us (21%)
  blocking collectives  72.4 us (12%)
  starting transfers between devices  38 us (7%)
  other arithmetic  16.3 us (3%)
  between operations  15.6 us (3%)
    psum x1, waiting for transfers between devices, per_device(): lax.psum((first_terms, second_terms, coarse_terms), ('dp', 'ty', 'tz'))  141 us
    unnamed x290, local copies, waits for them, and re-layouts  89.9 us
    psum x1, blocking collectives, per_device(): lax.psum((first_terms, second_terms, coarse_terms), ('dp', 'ty', 'tz'))  72.4 us
    dot_general x27, matrix products, transposed_last(): jnp.einsum('bxyzo,oc->bxyzc', window, weight[9 * sx + 3 * sy + sz], prefe...  49.7 us
    dot_general x54, matrix products, weight_grad(): jnp.einsum('boxyz,bcxyz->oc', cotangent, window, preferred_element_type=j...  39.1 us
    ppermute x6, starting transfers between devices, with_halo(): lax.ppermute(tail, axis, [(i, (i + 1) % count) for i in range(ends)])  27.8 us
    dot_general x54, matrix products, transposed_conv(): jnp.einsum('oc,boxyz->bcxyz', weight[9 * sx + 3 * sy + sz], window, prefe...  25.7 us
    dot_general x27, matrix products, weight_grad_last(): jnp.einsum('bxyzo,bxyzc->oc', cotangent, window, preferred_element_type=j...  25.3 us
  transfers between devices with their start and end apart: 13, of which 2 were waited for; matrix products, arithmetic and copies ran while one was open for 37% of the time, Pallas kernels for 0%

commit v1 on v0

v1 whole, which is shorter than its diff:
```python
import functools

import jax
import jax.numpy as jnp
from jax import lax
from jax.experimental import pallas as pl
from jax.experimental.pallas import tpu as pltpu
from jax.sharding import PartitionSpec as P

MESH = pl.DeviceIdType.MESH
BF = jnp.bfloat16
F32 = jnp.float32
NN = (((1,), (0,)), ((), ()))
NT = (((1,), (1,)), ((), ()))
TN = (((0,), (0,)), ((), ()))
ROWS = 34 * 32
C0 = 0.7978845608028654
C1 = 0.044715


def mm(a, b, dims=NN):
    return lax.dot_general(a, b, dims, preferred_element_type=F32)


def iota(shape, dim):
    return lax.broadcasted_iota(jnp.int32, shape, dim)


def one_hot(cond):
    return jnp.where(cond, 1.0, 0.0).astype(BF)


def kernel(
    sizes,
    fin,
    fcot,
    w1,
    w1t,
    w2t,
    cin,
    ccot,
    wc,
    o_gfi,
    o_gf,
    o_gs,
    o_gci,
    o_gc,
    perm,
    shifts,
    xin,
    xcot,
    xdp,
    act,
    bands,
    ysend,
    yrecv,
    zsend,
    zrecv,
    dsend,
    drecv,
    ysend2,
    yrecv2,
    zsend2,
    zrecv2,
    cflat,
    cplus,
    cminus,
    vmat,
    inp3,
    rsend,
    rs1,
    qf,
    qb,
    rs2,
    acc1,
    acc2,
    fpart,
    ar1,
    fsum1,
    ar2,
    fsum2,
    gath,
    hs,
    hr,
    gs,
    gr,
    r1s,
    r1r,
    r2s,
    r2r,
    a1s,
    a1r,
    a2s,
    a2r,
    a3s,
    a3r,
):
    ndp, nty, ntz = sizes
    dp, ty, tz = lax.axis_index("dp"), lax.axis_index("ty"), lax.axis_index("tz")
    zgroup = ndp * ntz
    me = dp * ntz + tz

    def at(dy, dz):
        return (dp, lax.rem(ty + dy + nty, nty), lax.rem(tz + dz + ntz, ntz))

    def ty_peer(j):
        t = lax.rem(ty + j, nty)
        return t, (dp, t, tz)

    def z_peer(j):
        g = lax.rem(me + j, zgroup)
        z = lax.rem(g, ntz)
        return g, z, (lax.div(g, ntz), ty, z)

    def remote(src, dst, ssem, rsem, dev):
        return pltpu.make_async_remote_copy(
            src_ref=src,
            dst_ref=dst,
            send_sem=ssem,
            recv_sem=rsem,
            device_id=dev,
            device_id_type=MESH,
        )

    up = (ty > 0, ty < nty - 1)
    side = (tz > 0, tz < ntz - 1)

    barrier = pltpu.get_barrier_semaphore()
    partners = [at(dy, dz) for dy in (-1, 1) for dz in (-1, 1)]
    partners += [ty_peer(j)[1] for j in range(1, nty)]
    partners += [z_peer(j)[2] for j in range(1, zgroup)]
    for dev in partners:
        pl.semaphore_signal(barrier, inc=1, device_id=dev, device_id_type=MESH)

    r, c = iota((512, 512), 0), iota((512, 512), 1)
    perm[...] = one_hot(c == (r % 16) * 32 + ((r // 16) % 2) * 16 + r // 32)
    r, c = iota((128, 256), 0), iota((128, 256), 1)
    shifts[0] = one_hot(((r == c + 1) & (c < 127)) | ((r + 1 == c - 128) & (c > 128)))
    shifts[1] = one_hot((r == 0) & (c == 127))
    shifts[2] = one_hot((r == 127) & (c == 128))

    def relayout(src, dst):
        for j in range(2):
            left = src[:, 16 * j : 16 * j + 16, :].reshape(512, 128)
            right = src[:, 32 + 16 * j : 48 + 16 * j, :].reshape(512, 128)
            both = jnp.concatenate([left, right], 1)
            dst[0, 32 + 512 * j : 544 + 512 * j, :] = mm(perm[...], both).astype(BF)

    relayout(fin, xin)
    relayout(fcot, xcot)

    def pick(first):
        r, c = iota((16, 128), 0), iota((16, 128), 1)
        return one_hot(((r == first) & (c == 0)) | ((r == first + 1) & (c == 127)))

    for h in range(2):
        lanes = slice(128 * h, 128 * h + 128)
        edge = mm(pick(0), xin[0, 32:1056, lanes], NT) + mm(pick(2), xcot[0, 32:1056, lanes], NT)
        edge = edge.astype(BF)
        for j in range(8):
            rows = slice((8 * h + j) * 16, (8 * h + j) * 16 + 16)
            tile = edge[:, 128 * j : 128 * j + 128]
            zsend[0, rows, :] = tile
            zsend[1, rows, :] = tile

    for x in range(16):
        cflat[80 * x + 8 : 80 * x + 72, :] = ccot[64 * x : 64 * x + 64, :].astype(F32)

    def column(y, z):
        return cflat[pl.ds(8 * y + z, 16, stride=80), :]

    for y in range(8):
        zsend[0, 256 + 16 * y : 272 + 16 * y, :] = column(y + 1, 0).astype(BF)
        zsend[1, 256 + 16 * y : 272 + 16 * y, :] = column(y + 1, 7).astype(BF)
    for s in range(2):
        own = (slice(32, 64), slice(0, 128)) if s == 0 else (slice(1024, 1056), slice(128, 256))
        e_in, e_cot = xin[(0, *own)], xcot[(0, *own)]
        ysend[s, 0:32, :] = e_in
        ysend[s, 32:64, :] = e_cot
        first = 8 if s == 0 else 64
        for x in range(0, 16, 2):
            pair = [cflat[80 * (x + q) + first : 80 * (x + q) + first + 8, :] for q in range(2)]
            ysend[s, 64 + 8 * x : 80 + 8 * x, :] = jnp.concatenate(pair, 0).astype(BF)
        for t in range(2):
            dsend[s, t, 0:32, :] = e_in
            dsend[s, t, 32:64, :] = e_cot
            dsend[s, t, 64:80, :] = column(1 if s == 0 else 8, 0 if t == 0 else 7).astype(BF)

    pl.semaphore_wait(barrier, len(partners))

    step = (-1, 1)
    halo = []
    for s in range(2):
        halo.append(remote(ysend.at[s], yrecv.at[s], hs.at[s], hr.at[s], at(step[s], 0)))
        halo.append(remote(zsend.at[s], zrecv.at[s], hs.at[2 + s], hr.at[2 + s], at(0, step[s])))
        for t in range(2):
            q = 4 + 2 * s + t
            halo.append(
                remote(dsend.at[s, t], drecv.at[s, t], hs.at[q], hr.at[q], at(step[s], step[t]))
            )
    for copy in halo:
        copy.start()

    rl = one_hot(iota((16, 256), 1) % 16 == iota((16, 256), 0))
    lane = iota((16, 256), 1)
    for n, w in enumerate((w1, w2t, w1t)):
        wide = mm(w[...], rl)
        for cc in range(3):
            for xo in range(2):
                strip = jnp.zeros((16, 256), F32)
                for b in range(3):
                    for xi in range(2):
                        k = 9 * (xi - xo + 1) + 3 * b + cc
                        strip = jnp.where(
                            lane // 16 == 2 * b + xi, wide[16 * k : 16 * k + 16, :], strip
                        )
                for yo in range(4):
                    moved = strip if yo == 0 else pltpu.roll(strip, 32 * yo, 1)
                    first = 32 * yo + 16 * xo
                    bands[n, cc, first : first + 16, :] = moved.astype(BF)

    inp3[...] = jnp.zeros_like(inp3)
    for a in range(3):
        inp3[64 * (2 - a) : 64 * (2 - a) + 1024, 128 * a : 128 * a + 128] = cin[...]
    vmat[0] = jnp.zeros((64, 1152), BF)
    vmat[17] = jnp.zeros((64, 1152), BF)
    qf[...] = jnp.zeros_like(qf)

    for copy in halo:
        copy.wait()

    def valid(cond, value):
        return jnp.where(cond, value, jnp.zeros_like(value))

    for x in range(16):
        rows = slice(64 + 8 * (x // 2 * 2), 80 + 8 * (x // 2 * 2))
        half = slice(8 * (x % 2), 8 * (x % 2) + 8)
        cflat[80 * x : 80 * x + 8, :] = valid(up[0], yrecv[1, rows, :].astype(F32)[half])
        cflat[80 * x + 72 : 80 * x + 80, :] = valid(up[1], yrecv[0, rows, :].astype(F32)[half])
    cplus[...] = pltpu.roll(cflat[...], 1279, 0)
    cminus[...] = pltpu.roll(cflat[...], 1, 0)
    for y in range(10):
        for ref, z, t, ok in ((cplus, 7, 0, side[1]), (cminus, 0, 1, side[0])):
            if y == 0:
                part, ok = drecv[1, t, 64:80, :], ok & up[0]
            elif y == 9:
                part, ok = drecv[0, t, 64:80, :], ok & up[1]
            else:
                part = zrecv[t, 256 + 16 * (y - 1) : 272 + 16 * (y - 1), :]
            ref[pl.ds(8 * y + z, 16, stride=80), :] = valid(ok, part.astype(F32))

    def spread(x, carry):
        for b in range(3):
            for cc, ref in enumerate((cplus, cflat, cminus)):
                rows = ref[pl.ds(pl.multiple_of(x * 80 + 8 * (2 - b), 8), 64), :]
                q = 3 * b + cc
                vmat[x + 1, :, 128 * q : 128 * q + 128] = rows.astype(BF)
        return carry

    lax.fori_loop(0, 16, spread, 0)

    for b in range(3):
        left = vmat[:, :, 384 * b : 384 * b + 384].reshape(1152, 384)
        g = mm(left, inp3[...], TN)
        for cc in range(3):
            for a in range(3):
                rsend[9 * a + 3 * b + cc] = g[
                    128 * cc : 128 * cc + 128, 128 * a : 128 * a + 128
                ].astype(BF)
    wide_o = 128 // nty

    def part1(t):
        return rsend.at[:, pl.ds(pl.multiple_of(t * wide_o, 16), wide_o), :]

    hop1 = []
    for j in range(1, nty):
        t, dev = ty_peer(j)
        hop1.append(remote(part1(t), rs1.at[ty], r1s.at[j], r1r.at[nty - j], dev))
    for copy in hop1:
        copy.start()

    def fill(dst, first, get_y, get_d, get_z):
        pieces, halves = [], []
        for s in (1, 0):
            ok = up[0] if s == 1 else up[1]
            mid = valid(ok, get_y(s))
            after, before = valid(ok & side[1], get_d(s, 0)), valid(ok & side[0], get_d(s, 1))
            out = mm(mid, shifts[0]) + mm(after, shifts[1]) + mm(before, shifts[2])
            rows, lanes = (slice(0, 32), slice(0, 128)) if s == 1 else (slice(1056, 1088), slice(128, 256))
            dst[0, rows, lanes] = mid
            dst[2, rows, lanes] = out[:, :128].astype(BF)
            dst[1, rows, lanes] = out[:, 128:].astype(BF)
        r, c = iota((32, 256), 0), iota((32, 256), 1)
        place = one_hot(
            ((r == first) & (c == 127) & side[1]) | ((r == 17 + first) & (c == 128) & side[0])
        )
        for h in range(2):
            lanes = slice(128 * h, 128 * h + 128)
            for j in range(8):
                rows = slice(32 + 128 * j, 160 + 128 * j)
                got = slice((8 * h + j) * 16, (8 * h + j) * 16 + 16)
                edge = jnp.concatenate([get_z(0, got), get_z(1, got)], 0)
                out = mm(dst[0, rows, lanes], shifts[0]) + mm(edge, place, TN)
                dst[2, rows, lanes] = out[:, :128].astype(BF)
                dst[1, rows, lanes] = out[:, 128:].astype(BF)
        for v in range(3):
            dst[v, 0:32, 128:256] = dst[v, 1024:1056, 0:128]
            dst[v, 1056:1088, 0:128] = dst[v, 32:64, 128:256]

    for n, dst in enumerate((xin, xcot)):
        rows = slice(32 * n, 32 * n + 32)
        fill(
            dst,
            2 * n,
            lambda s, rows=rows: yrecv[s, rows, :],
            lambda s, t, rows=rows: drecv[s, t, rows, :],
            lambda t, got: zrecv[t, got, :],
        )

    version = (1, 0, 2)

    def conv(n, src, g):
        rows = pl.ds(pl.multiple_of(g * 128, 128), 192)
        out = None
        for cc in range(3):
            term = mm(bands[n, cc, :, 0:192], src[version[cc], rows, :])
            out = term if out is None else out + term
        return out

    def forward(g, carry):
        pre = conv(0, xin, g)
        dact = conv(1, xcot, g)
        square = pre * pre
        t = jnp.tanh(C0 * pre * (1.0 + C1 * square))
        half = 0.5 + 0.5 * t
        slope = half + 0.5 * pre * (1.0 - t * t) * (C0 * (1.0 + (3.0 * C1) * square))
        act[pl.ds(pl.multiple_of(g * 128, 128), 128), :] = (pre * half).astype(BF)
        xdp[0, pl.ds(pl.multiple_of(g * 128 + 32, 32), 128), :] = (dact * slope).astype(BF)
        return carry

    lax.fori_loop(0, 8, forward, 0)

    for h in range(2):
        lanes = slice(128 * h, 128 * h + 128)
        edge = mm(pick(0), xdp[0, 32:1056, lanes], NT).astype(BF)
        for j in range(8):
            rows = slice((8 * h + j) * 16, (8 * h + j) * 16 + 16)
            zsend2[rows, :] = edge[:, 128 * j : 128 * j + 128]
    ysend2[0] = xdp[0, 32:64, 0:128]
    ysend2[1] = xdp[0, 1024:1056, 128:256]
    halo2 = []
    for s in range(2):
        halo2.append(remote(ysend2.at[s], yrecv2.at[s, 0], gs.at[s], gr.at[s], at(step[s], 0)))
        halo2.append(remote(zsend2, zrecv2.at[s], gs.at[2 + s], gr.at[2 + s], at(0, step[s])))
        for t in range(2):
            q = 4 + 2 * s + t
            halo2.append(
                remote(ysend2.at[s], yrecv2.at[s, 1 + t], gs.at[q], gr.at[q], at(step[s], step[t]))
            )
    for copy in halo2:
        copy.start()

    acc1[...] = jnp.zeros_like(acc1)
    acc2[...] = jnp.zeros_like(acc2)

    def gram(g, carry):
        rows = pl.ds(pl.multiple_of(g * 128, 128), 192)
        own = xdp[0, pl.ds(pl.multiple_of(g * 128 + 32, 32), 128), :]
        a_own = act[pl.ds(pl.multiple_of(g * 128, 128), 128), :]
        for cc in range(3):
            acc1[cc, :, 0:192] += mm(own, xin[version[cc], rows, :], NT)
            acc2[cc] += mm(xcot[version[cc], rows, :], a_own, NT)
        return carry

    lax.fori_loop(0, 8, gram, 0)
    for cc in range(3):
        total = None
        for yo in range(4):
            part = acc1[cc, 32 * yo : 32 * yo + 32, :]
            part = part if yo == 0 else pltpu.roll(part, 256 - 32 * yo, 1)
            total = part if total is None else total + part
        fpart[32 * cc : 32 * cc + 32, :] = total[:, 0:128]
    total = jnp.zeros((96, 128), F32)
    lane = iota((96, 128), 1)
    for cc in range(3):
        band = None
        for yo in range(4):
            part = acc2[cc, 32 * yo : 32 * yo + 96, :]
            turn = (32 * cc - 32 * yo) % 128
            part = part if turn == 0 else pltpu.roll(part, turn, 1)
            band = part if band is None else band + part
        total = jnp.where(lane // 32 == cc, band, total)
    fpart[96:192, :] = total

    slab = 192 // nty
    hop_a = []
    for j in range(1, nty):
        t, dev = ty_peer(j)
        src = fpart.at[pl.ds(pl.multiple_of(t * slab, 8), slab), :]
        hop_a.append(remote(src, ar1.at[ty], a1s.at[j], a1r.at[nty - j], dev))
    for copy in hop_a:
        copy.start()
    ar1[ty] = fpart[pl.ds(pl.multiple_of(ty * slab, 8), slab), :]

    rs1[ty] = rsend[:, pl.ds(pl.multiple_of(ty * wide_o, 16), wide_o), :]
    for copy in hop1:
        copy.wait()

    def sum1(k, carry):
        total = rs1[0, k].astype(F32)
        for t in range(1, nty):
            total = total + rs1[t, k].astype(F32)
        qf[pl.ds(k, wide_o, stride=32), :] = total
        return carry

    lax.fori_loop(0, 27, sum1, 0)
    qb[...] = qf[...].astype(BF)
    deep = 32 * wide_o // ntz

    hop2 = []
    for j in range(1, zgroup):
        g, z, dev = z_peer(j)
        src = qb.at[pl.ds(pl.multiple_of(z * deep, 16), deep), :]
        hop2.append(remote(src, rs2.at[me], r2s.at[j], r2r.at[zgroup - j], dev))
    for copy in hop2:
        copy.start()
    rs2[me] = qb[pl.ds(pl.multiple_of(tz * deep, 16), deep), :]

    for copy in hop_a:
        copy.wait()
    total = ar1[0]
    for t in range(1, nty):
        total = total + ar1[t]
    fsum1[...] = total
    hop_b = []
    for j in range(1, zgroup):
        g, z, dev = z_peer(j)
        hop_b.append(remote(fsum1, ar2.at[me], a2s.at[j], a2r.at[zgroup - j], dev))
    for copy in hop_b:
        copy.start()
    ar2[me] = fsum1[...]

    def coarse(q, carry):
        out = None
        for a in range(3):
            left = vmat[pl.ds(q * 4 + 2 - a, 4)].reshape(256, 1152)
            term = mm(left, wc[1152 * a : 1152 * a + 1152, :])
            out = term if out is None else out + term
        o_gci[pl.ds(pl.multiple_of(q * 256, 256), 256), :] = out.astype(BF)
        return carry

    lax.fori_loop(0, 4, coarse, 0)

    for copy in hop_b:
        copy.wait()
    total = ar2[0]
    for t in range(1, zgroup):
        total = total + ar2[t]
    fsum2[...] = total
    hop_c = []
    for j in range(1, nty):
        t, dev = ty_peer(j)
        hop_c.append(remote(fsum2, gath.at[ty], a3s.at[j], a3r.at[nty - j], dev))
    for copy in hop_c:
        copy.start()
    gath[ty] = fsum2[...]

    for copy in halo2:
        copy.wait()
    fill(
        xdp,
        0,
        lambda s: yrecv2[s, 0],
        lambda s, t: yrecv2[s, 1 + t],
        lambda t, got: zrecv2[t, got, :],
    )

    def last(j, carry):
        parts = [conv(2, xdp, 4 * j + q).astype(BF) for q in range(4)]
        out = mm(perm[...], jnp.concatenate(parts, 0)).astype(BF)
        first = pl.multiple_of(16 * j, 16)
        o_gfi[:, pl.ds(first, 16), :] = out[:, :128].reshape(32, 16, 128)
        o_gfi[:, pl.ds(first + 32, 16), :] = out[:, 128:].reshape(32, 16, 128)
        return carry

    lax.fori_loop(0, 2, last, 0)

    for copy in hop2:
        copy.wait()
    total = rs2[0].astype(F32)
    for t in range(1, zgroup):
        total = total + rs2[t].astype(F32)
    for o in range(wide_o // ntz):
        o_gc[o] = total[32 * o : 32 * o + 27, :]

    for copy in hop_c:
        copy.wait()
    fpart[...] = gath[...].reshape(192, 128)
    for a in range(3):
        planes = [(xo, xo + a - 1) for xo in range(2) if 0 <= xo + a - 1 < 2]
        for b in range(3):
            for cc in range(3):
                k = 9 * a + 3 * b + cc
                one, two = None, None
                for xo, xi in planes:
                    first = 32 * cc + 16 * xo
                    lanes = slice(32 * b + 16 * xi, 32 * b + 16 * xi + 16)
                    part = fpart[first : first + 16, lanes]
                    one = part if one is None else one + part
                    first = 96 + 32 * b + 16 * xi
                    lanes = slice(32 * cc + 16 * xo, 32 * cc + 16 * xo + 16)
                    part = fpart[first : first + 16, lanes]
                    two = part if two is None else two + part
                o_gf[k] = one
                o_gs[26 - k] = two


def solution(mesh):
    sizes = tuple(mesh.shape[a] for a in ("dp", "ty", "tz"))
    ndp, nty, ntz = sizes
    zgroup = ndp * ntz
    wide_o = 128 // nty
    slab = 192 // nty

    def per_device(fine_input, fine_cotangent, first_weight, second_weight, coarse_input, coarse_cotangent, coarse_weight):
        def turned(w):
            return w[::-1].transpose(0, 2, 1).reshape(432, 16)

        dma = pltpu.SemaphoreType.DMA
        scratch = [
            pltpu.VMEM((512, 512), BF),
            pltpu.VMEM((3, 128, 256), BF),
            pltpu.VMEM((3, ROWS, 256), BF),
            pltpu.VMEM((3, ROWS, 256), BF),
            pltpu.VMEM((3, ROWS, 256), BF),
            pltpu.VMEM((1024, 256), BF),
            pltpu.VMEM((3, 3, 128, 256), BF),
            pltpu.VMEM((2, 192, 128), BF),
            pltpu.VMEM((2, 192, 128), BF),
            pltpu.VMEM((2, 384, 128), BF),
            pltpu.VMEM((2, 384, 128), BF),
            pltpu.VMEM((2, 2, 80, 128), BF),
            pltpu.VMEM((2, 2, 80, 128), BF),
            pltpu.VMEM((2, 32, 128), BF),
            pltpu.VMEM((2, 3, 32, 128), BF),
            pltpu.VMEM((256, 128), BF),
            pltpu.VMEM((2, 256, 128), BF),
            pltpu.VMEM((1280, 128), F32),
            pltpu.VMEM((1280, 128), F32),
            pltpu.VMEM((1280, 128), F32),
            pltpu.VMEM((18, 64, 1152), BF),
            pltpu.VMEM((1152, 384), BF),
            pltpu.VMEM((27, 128, 128), BF),
            pltpu.VMEM((nty, 27, wide_o, 128), BF),
            pltpu.VMEM((32 * wide_o, 128), F32),
            pltpu.VMEM((32 * wide_o, 128), BF),
            pltpu.VMEM((zgroup, 32 * wide_o // ntz, 128), BF),
            pltpu.VMEM((3, 128, 256), F32),
            pltpu.VMEM((3, 192, 128), F32),
            pltpu.VMEM((192, 128), F32),
            pltpu.VMEM((nty, slab, 128), F32),
            pltpu.VMEM((slab, 128), F32),
            pltpu.VMEM((zgroup, slab, 128), F32),
            pltpu.VMEM((slab, 128), F32),
            pltpu.VMEM((nty, slab, 128), F32),
            dma((8,)),
            dma((8,)),
            dma((8,)),
            dma((8,)),
            dma((nty,)),
            dma((nty,)),
            dma((zgroup,)),
            dma((zgroup,)),
            dma((nty,)),
            dma((nty,)),
            dma((zgroup,)),
            dma((zgroup,)),
            dma((nty,)),
            dma((nty,)),
        ]
        vmem = pl.BlockSpec(memory_space=pltpu.VMEM)
        outs = pl.pallas_call(
            functools.partial(kernel, sizes),
            out_shape=(
                jax.ShapeDtypeStruct((32, 64, 128), BF),
                jax.ShapeDtypeStruct((27, 16, 16), F32),
                jax.ShapeDtypeStruct((27, 16, 16), F32),
                jax.ShapeDtypeStruct((1024, 128), BF),
                jax.ShapeDtypeStruct((wide_o // ntz, 27, 128), F32),
            ),
            in_specs=[vmem] * 8,
            out_specs=(vmem,) * 5,
            scratch_shapes=scratch,
            compiler_params=pltpu.CompilerParams(
                collective_id=0, has_side_effects=True, vmem_limit_bytes=48 * 1024 * 1024
            ),
        )(
            fine_input.reshape(32, 64, 128),
            fine_cotangent.reshape(32, 64, 128),
            first_weight.reshape(432, 16),
            turned(first_weight),
            turned(second_weight),
            coarse_input.reshape(1024, 128),
            coarse_cotangent.reshape(1024, 128),
            coarse_weight.reshape(3456, 128),
        )
        return (
            outs[0].reshape(fine_input.shape),
            outs[1],
            outs[2],
            outs[3].reshape(coarse_input.shape),
            outs[4],
        )

    fine = P("dp", None, None, "ty", "tz")
    wide = P("dp", None, "ty", "tz", None)
    return jax.shard_map(
        per_device,
        mesh=mesh,
        in_specs=(fine, fine, P(), P(), wide, wide, P()),
        out_specs=(fine, P(), P(), wide, P(("ty", "tz"), None, None)),
        check_vma=False,
    )
```

time: 583 us -> 55.7 us (0.10); the launches traced: 576 us -> 55.3 us
  matrix products: 164 us -> 0 us
  waiting for transfers between devices: 145 us -> 0 us
  local copies, waits for them, and re-layouts: 124 us -> 10.4 us
  blocking collectives: 72.4 us -> 0 us
  Pallas kernels: 0 us -> 44.3 us
  starting transfers between devices: 38 us -> 0 us
  other arithmetic: 16.3 us -> 0 us
  between operations: 15.6 us -> 0.7 us
    dot_general x189 -> x0, matrix products: 164 us -> none  [the longest x27 49.7 us: transposed_last(): jnp.einsum('bxyzo,oc->bxyzc', window, weight[9 * sx + 3 * sy + sz], prefe...]
    psum x1 -> x0, waiting for transfers between devices: 141 us -> none  [per_device(): lax.psum((first_terms, second_terms, coarse_terms), ('dp', 'ty', 'tz'))]
    unnamed x290 -> x16, local copies, waits for them, and re-layouts: 89.9 us -> 7.99 us
    psum x1 -> x0, blocking collectives: 72.4 us -> none  [per_device(): lax.psum((first_terms, second_terms, coarse_terms), ('dp', 'ty', 'tz'))]
    pallas_call x0 -> x1, Pallas kernels: none -> 44.3 us  [per_device(): pl.pallas_call(functools.partial(kernel, sizes), out_shape=(jax.ShapeDtyp...]
    ppermute x12 -> x0, starting transfers between devices: 38 us -> none  [the longest x6 27.8 us: with_halo(): lax.ppermute(tail, axis, [(i, (i + 1) % count) for i in range(ends)])]
    slice x14 -> x0, local copies, waits for them, and re-layouts: 19.3 us -> none  [the longest x6 10.2 us: with_halo(): lax.slice_in_dim(cells, cells.shape[dim] - width, cells.shape[dim], axis=...]
    concatenate x8 -> x0, other arithmetic: 15.2 us -> none  [with_halo(): jnp.concatenate([lax.ppermute(tail, axis, [(i, (i + 1) % count) for i in...]
  transfers between devices with their start and end apart: 13 -> 0, of which waited for: 2 -> 0; matrix products, arithmetic and copies ran while one was open for 37% -> 0% of each run, Pallas kernels for 0% -> 0%
where the time goes in v1:
time: 55.7 us; the launch traced here: 55.3 us
  Pallas kernels  44.3 us (80%)
  local copies, waits for them, and re-layouts  10.4 us (19%)
  between operations  0.7 us (1%)
    pallas_call x1, Pallas kernels, per_device(): pl.pallas_call(functools.partial(kernel, sizes), out_shape=(jax.ShapeDtyp...  44.3 us
    unnamed x16, local copies, waits for them, and re-layouts  7.99 us
    rev x2, local copies, waits for them, and re-layouts, turned(): return w[::-1].transpose(0, 2, 1).reshape(432, 16)  1.97 us

profile of v1, /device:TPU:1, one launch (start us, length us, event | category | flops | bytes accessed | tf_op | source)
XLA Modules:
  0.0 55.3 jit_solution(18134717926472089430)
XLA Ops:
  0.6 0.0 copy-start.1
  0.6 1.0 %rev.7 = bf16[27,16,16]{0,2,1:T(8,128)(2,1)S(1)} reverse(bf16[27,16,16]{0,2,1:T(8,128)(2,1)} %param.10), dimensions={0} | reverse | bytes 27648 | tf_op jit(solution)/shard_map/rev | solution.py:527
  1.6 0.2 copy.14
  1.8 0.0 copy-start.3
  1.9 1.0 %rev.6 = bf16[27,16,16]{0,2,1:T(8,128)(2,1)S(1)} reverse(bf16[27,16,16]{0,2,1:T(8,128)(2,1)} %param.9), dimensions={0} | reverse | bytes 27648 | tf_op jit(solution)/shard_map/rev | solution.py:527
  2.8 0.2 copy.13
  3.0 1.0 %copy.12 = bf16[27,16,16]{2,1,0:T(8,128)(2,1)S(1)} copy(bf16[27,16,16]{0,2,1:T(8,128)(2,1)} %param.9) | data formatting | bytes 27648 | tf_op args[2]
  4.1 0.0 copy-done.1
  4.1 0.0 copy-done.3
  4.1 0.0 copy-start
  4.1 1.2 %copy-done = bf16[27,128,128]{2,1,0:T(8,128)(2,1)S(1)} copy-done((bf16[27,128,128]{2,1,0:T(8,128)(2,1)S(1)}, bf16[27,128,128]{2,1,0:T(8,128)(2,1)}, u32[]{:S(2)}) %copy-start) | copy-done | bytes 884760
  5.3 0.0 copy-start.2
  5.3 1.0 %copy-done.2 = bf16[1,16,2,64,128]{4,3,2,1,0:T(8,128)(2,1)S(1)} copy-done((bf16[1,16,2,64,128]{4,3,2,1,0:T(8,128)(2,1)S(1)}, bf16[1,16,2,64,128]{4,3,2,1,0:T(8,128)(2,1)}, u32[]{:S(2)}) %copy-start.2) | copy-done | bytes 524312
  6.3 0.0 copy-start.4
  6.3 0.9 %copy-done.4 = bf16[1,16,8,8,128]{4,3,2,1,0:T(8,128)(2,1)S(1)} copy-done((bf16[1,16,8,8,128]{4,3,2,1,0:T(8,128)(2,1)S(1)}, bf16[1,16,8,8,128]{4,3,2,1,0:T(8,128)(2,1)}, u32[]{:S(2)}) %copy-start.4) | copy-done | bytes 262168
  7.3 44.3 %shard_map.110 = (bf16[32,64,128]{2,1,0:T(8,128)(2,1)S(1)}, f32[27,16,16]{2,1,0:T(8,128)S(1)}, f32[27,16,16]{2,1,0:T(8,128)S(1)}, bf16[1024,128]{1,0:T(8,128)(2,1)S(1)}, f32[2,27,128]{2,1,0:T(8,128)S(1)}) custom-call(bf16[32,64,128]{2,1,0:T(8,128)(2,1)S(1)} %bitcast.14, bf16[32,64,128]{2,1,0:T(8,128)(2,1)S(1)} %bitcast.15, bf16[432,16]{1,0:T(8,128)(2,1)S(1)} %bitcast.18, ...), custom_call_target="tpu_custom_call" | custom-call | tf_op jit(solution)/shard_map/pallas_call | solution.py:582
  51.5 0.6 %copy.17 = f32[2,27,128]{2,0,1:T(2,128)} copy(f32[2,27,128]{2,1,0:T(8,128)S(1)} %get-tuple-element.19) | data formatting | bytes 55296
  52.2 0.8 %copy.15 = f32[27,16,16]{0,2,1:T(8,128)} copy(f32[27,16,16]{2,1,0:T(8,128)S(1)} %get-tuple-element.16) | data formatting | bytes 55296
  53.0 0.8 %copy.16 = f32[27,16,16]{0,2,1:T(8,128)} copy(f32[27,16,16]{2,1,0:T(8,128)S(1)} %get-tuple-element.17) | data formatting | bytes 55296
  53.8 0.8 %copy.20 = bf16[1,16,2,64,128]{4,3,2,1,0:T(8,128)(2,1)} copy(bf16[1,16,2,64,128]{4,3,2,1,0:T(8,128)(2,1)S(1)} %bitcast.13) | data formatting | bytes 1048576
  54.6 0.7 %copy.21 = bf16[1,16,8,8,128]{4,3,2,1,0:T(8,128)(2,1)} copy(bf16[1,16,8,8,128]{4,3,2,1,0:T(8,128)(2,1)S(1)} %bitcast.19) | data formatting | bytes 524288
Async XLA Ops:
  0.6 3.4 %copy-start.1 = (bf16[1,16,2,64,128]{4,3,2,1,0:T(8,128)(2,1)S(1)}, bf16[1,16,2,64,128]{4,3,2,1,0:T(8,128)(2,1)}, u32[]{:S(2)}) copy-start(bf16[1,16,2,64,128]{4,3,2,1,0:T(8,128)(2,1)} %param.7) | copy-start | bytes 1572868
  1.8 2.2 %copy-start.3 = (bf16[1,16,8,8,128]{4,3,2,1,0:T(8,128)(2,1)S(1)}, bf16[1,16,8,8,128]{4,3,2,1,0:T(8,128)(2,1)}, u32[]{:S(2)}) copy-start(bf16[1,16,8,8,128]{4,3,2,1,0:T(8,128)(2,1)} %param.11) | copy-start | bytes 786436
  4.1 1.2 %copy-start = (bf16[27,128,128]{2,1,0:T(8,128)(2,1)S(1)}, bf16[27,128,128]{2,1,0:T(8,128)(2,1)}, u32[]{:S(2)}) copy-start(bf16[27,128,128]{2,1,0:T(8,128)(2,1)} %param.13) | copy-start | bytes 2654212
  5.3 1.0 %copy-start.2 = (bf16[1,16,2,64,128]{4,3,2,1,0:T(8,128)(2,1)S(1)}, bf16[1,16,2,64,128]{4,3,2,1,0:T(8,128)(2,1)}, u32[]{:S(2)}) copy-start(bf16[1,16,2,64,128]{4,3,2,1,0:T(8,128)(2,1)} %param.8) | copy-start | bytes 1572868
  6.3 0.9 %copy-start.4 = (bf16[1,16,8,8,128]{4,3,2,1,0:T(8,128)(2,1)S(1)}, bf16[1,16,8,8,128]{4,3,2,1,0:T(8,128)(2,1)}, u32[]{:S(2)}) copy-start(bf16[1,16,8,8,128]{4,3,2,1,0:T(8,128)(2,1)} %param.12) | copy-start | bytes 786436

commit v2 on v1

--- a/solution.py
+++ b/solution.py
@@ -32,19 +32,25 @@
 
 def kernel(
     sizes,
-    fin,
-    fcot,
-    w1,
-    w1t,
-    w2t,
-    cin,
-    ccot,
-    wc,
+    h_fin,
+    h_fcot,
+    h_w1,
+    h_w2,
+    h_cin,
+    h_ccot,
+    h_wc,
     o_gfi,
     o_gf,
     o_gs,
     o_gci,
     o_gc,
+    fin,
+    fcot,
+    w1,
+    w2,
+    cin,
+    ccot,
+    wc,
     perm,
     shifts,
     xin,
@@ -62,12 +68,15 @@
     yrecv2,
     zsend2,
     zrecv2,
+    drecv2,
     cflat,
     cplus,
     cminus,
     vmat,
     inp3,
     rsend,
+    rpair,
+    psum,
     rs1,
     qf,
     qb,
@@ -80,8 +89,11 @@
     ar2,
     fsum2,
     gath,
+    ls,
     hs,
     hr,
+    ps,
+    pr,
     gs,
     gr,
     r1s,
@@ -122,6 +134,12 @@
             device_id_type=MESH,
         )
 
+    loads = []
+    pairs = ((h_ccot, ccot), (h_fin, fin), (h_fcot, fcot), (h_w1, w1), (h_w2, w2), (h_cin, cin), (h_wc, wc))
+    for n, (src, dst) in enumerate(pairs):
+        loads.append(pltpu.make_async_copy(src, dst, ls.at[n]))
+        loads[n].start()
+
     up = (ty > 0, ty < nty - 1)
     side = (tz > 0, tz < ntz - 1)
 
@@ -135,9 +153,7 @@
     r, c = iota((512, 512), 0), iota((512, 512), 1)
     perm[...] = one_hot(c == (r % 16) * 32 + ((r // 16) % 2) * 16 + r // 32)
     r, c = iota((128, 256), 0), iota((128, 256), 1)
-    shifts[0] = one_hot(((r == c + 1) & (c < 127)) | ((r + 1 == c - 128) & (c > 128)))
-    shifts[1] = one_hot((r == 0) & (c == 127))
-    shifts[2] = one_hot((r == 127) & (c == 128))
+    shifts[...] = one_hot(((r == c + 1) & (c < 127)) | ((r + 1 == c - 128) & (c > 128)))
 
     def relayout(src, dst):
         for j in range(2):
@@ -146,23 +162,28 @@
             both = jnp.concatenate([left, right], 1)
             dst[0, 32 + 512 * j : 544 + 512 * j, :] = mm(perm[...], both).astype(BF)
 
+    def extract(src):
+        r, c = iota((32, 256), 0), iota((32, 256), 1)
+        total = None
+        for j in range(8):
+            sel = one_hot((r % 16 == 8 * (c // 128) + j) & (c % 128 == 127 * (r // 16)))
+            part = mm(sel, src[0, 32 + 128 * j : 160 + 128 * j, :], NT)
+            total = part if total is None else total + part
+        return total.astype(BF)
+
+    loads[1].wait()
     relayout(fin, xin)
+    loads[2].wait()
     relayout(fcot, xcot)
-
-    def pick(first):
-        r, c = iota((16, 128), 0), iota((16, 128), 1)
-        return one_hot(((r == first) & (c == 0)) | ((r == first + 1) & (c == 127)))
-
-    for h in range(2):
-        lanes = slice(128 * h, 128 * h + 128)
-        edge = mm(pick(0), xin[0, 32:1056, lanes], NT) + mm(pick(2), xcot[0, 32:1056, lanes], NT)
-        edge = edge.astype(BF)
-        for j in range(8):
-            rows = slice((8 * h + j) * 16, (8 * h + j) * 16 + 16)
-            tile = edge[:, 128 * j : 128 * j + 128]
-            zsend[0, rows, :] = tile
-            zsend[1, rows, :] = tile
-
+    for n, src in enumerate((xin, xcot)):
+        columns = extract(src)
+        for t in range(2):
+            tile = columns[16 * t : 16 * t + 16, :]
+            zsend[t, 16 * n : 16 * n + 16, :] = tile
+            for q in range(2):
+                dsend[q, t, 16 * n : 16 * n + 16, :] = tile
+
+    loads[0].wait()
     for x in range(16):
         cflat[80 * x + 8 : 80 * x + 72, :] = ccot[64 * x : 64 * x + 64, :].astype(F32)
 
@@ -170,21 +191,18 @@
         return cflat[pl.ds(8 * y + z, 16, stride=80), :]
 
     for y in range(8):
-        zsend[0, 256 + 16 * y : 272 + 16 * y, :] = column(y + 1, 0).astype(BF)
-        zsend[1, 256 + 16 * y : 272 + 16 * y, :] = column(y + 1, 7).astype(BF)
+        zsend[0, 32 + 16 * y : 48 + 16 * y, :] = column(y + 1, 0).astype(BF)
+        zsend[1, 32 + 16 * y : 48 + 16 * y, :] = column(y + 1, 7).astype(BF)
     for s in range(2):
         own = (slice(32, 64), slice(0, 128)) if s == 0 else (slice(1024, 1056), slice(128, 256))
-        e_in, e_cot = xin[(0, *own)], xcot[(0, *own)]
-        ysend[s, 0:32, :] = e_in
-        ysend[s, 32:64, :] = e_cot
+        ysend[s, 0:32, :] = xin[(0, *own)]
+        ysend[s, 32:64, :] = xcot[(0, *own)]
         first = 8 if s == 0 else 64
         for x in range(0, 16, 2):
             pair = [cflat[80 * (x + q) + first : 80 * (x + q) + first + 8, :] for q in range(2)]
             ysend[s, 64 + 8 * x : 80 + 8 * x, :] = jnp.concatenate(pair, 0).astype(BF)
         for t in range(2):
-            dsend[s, t, 0:32, :] = e_in
-            dsend[s, t, 32:64, :] = e_cot
-            dsend[s, t, 64:80, :] = column(1 if s == 0 else 8, 0 if t == 0 else 7).astype(BF)
+            dsend[s, t, 32:48, :] = column(1 if s == 0 else 8, 0 if t == 0 else 7).astype(BF)
 
     pl.semaphore_wait(barrier, len(partners))
 
@@ -201,25 +219,39 @@
     for copy in halo:
         copy.start()
 
-    rl = one_hot(iota((16, 256), 1) % 16 == iota((16, 256), 0))
-    lane = iota((16, 256), 1)
-    for n, w in enumerate((w1, w2t, w1t)):
-        wide = mm(w[...], rl)
+    lane = iota((32, 768), 1)
+    q, m = lane // 128, lane % 128
+    k = 9 * ((m // 16) % 2 - q % 2 + 1) + 3 * (m // 32) + q // 2
+    wanted = (m < 96, iota((32, 768), 0))
+    straight = one_hot(wanted[0] & (wanted[1] == k))[:27]
+    flipped = one_hot(wanted[0] & (wanted[1] == 26 - k))[:27]
+    r, c = iota((256, 768), 0), iota((256, 768), 1)
+    to_in, to_out = r % 16 == c % 16, r // 16 == c % 16
+    r, c = iota((16, 256), 0), iota((16, 256), 1)
+    by_out, by_in = one_hot(c // 16 == r), one_hot(c % 16 == r)
+    loads[3].wait()
+    loads[4].wait()
+    for n, (w, pick, mask, rows) in enumerate(
+        (
+            (w1, straight, to_in, by_out),
+            (w2, flipped, to_out, by_in),
+            (w1, flipped, to_out, by_in),
+        )
+    ):
+        wide = jnp.where(mask, mm(w[...], pick), 0.0).astype(BF)
+        strips = mm(rows, wide)
         for cc in range(3):
             for xo in range(2):
-                strip = jnp.zeros((16, 256), F32)
-                for b in range(3):
-                    for xi in range(2):
-                        k = 9 * (xi - xo + 1) + 3 * b + cc
-                        strip = jnp.where(
-                            lane // 16 == 2 * b + xi, wide[16 * k : 16 * k + 16, :], strip
-                        )
+                first = 128 * (2 * cc + xo)
+                strip = strips[:, first : first + 128]
+                strip = jnp.concatenate([strip, jnp.zeros_like(strip)], 1)
                 for yo in range(4):
                     moved = strip if yo == 0 else pltpu.roll(strip, 32 * yo, 1)
                     first = 32 * yo + 16 * xo
                     bands[n, cc, first : first + 16, :] = moved.astype(BF)
 
     inp3[...] = jnp.zeros_like(inp3)
+    loads[5].wait()
     for a in range(3):
         inp3[64 * (2 - a) : 64 * (2 - a) + 1024, 128 * a : 128 * a + 128] = cin[...]
     vmat[0] = jnp.zeros((64, 1152), BF)
@@ -242,11 +274,11 @@
     for y in range(10):
         for ref, z, t, ok in ((cplus, 7, 0, side[1]), (cminus, 0, 1, side[0])):
             if y == 0:
-                part, ok = drecv[1, t, 64:80, :], ok & up[0]
+                part, ok = drecv[1, t, 32:48, :], ok & up[0]
             elif y == 9:
-                part, ok = drecv[0, t, 64:80, :], ok & up[1]
+                part, ok = drecv[0, t, 32:48, :], ok & up[1]
             else:
-                part = zrecv[t, 256 + 16 * (y - 1) : 272 + 16 * (y - 1), :]
+                part = zrecv[t, 32 + 16 * (y - 1) : 48 + 16 * (y - 1), :]
             ref[pl.ds(8 * y + z, 16, stride=80), :] = valid(ok, part.astype(F32))
 
     def spread(x, carry):
@@ -259,48 +291,58 @@
 
     lax.fori_loop(0, 16, spread, 0)
 
+    wide_o, nx = 128 // nty, nty // 2
+    core, xme = lax.rem(ty, 2), lax.div(ty, 2)
+    other = (dp, ty + 1 - 2 * core, tz)
+    hop0 = []
     for b in range(3):
         left = vmat[:, :, 384 * b : 384 * b + 384].reshape(1152, 384)
         g = mm(left, inp3[...], TN)
-        for cc in range(3):
-            for a in range(3):
-                rsend[9 * a + 3 * b + cc] = g[
-                    128 * cc : 128 * cc + 128, 128 * a : 128 * a + 128
-                ].astype(BF)
-    wide_o = 128 // nty
-
-    def part1(t):
-        return rsend.at[:, pl.ds(pl.multiple_of(t * wide_o, 16), wide_o), :]
-
+        for a in range(3):
+            for cc in range(3):
+                part = g[128 * cc : 128 * cc + 128, 128 * a : 128 * a + 128]
+                rsend[9 * b + 3 * a + cc] = part.astype(BF).reshape(nx, 2, wide_o, 128)
+        src = rsend.at[pl.ds(9 * b, 9), :, 1 - core]
+        hop0.append(remote(src, rpair.at[pl.ds(9 * b, 9)], ps.at[b], pr.at[b], other))
+        hop0[b].start()
     hop1 = []
-    for j in range(1, nty):
-        t, dev = ty_peer(j)
-        hop1.append(remote(part1(t), rs1.at[ty], r1s.at[j], r1r.at[nty - j], dev))
-    for copy in hop1:
-        copy.start()
-
-    def fill(dst, first, get_y, get_d, get_z):
-        pieces, halves = [], []
+    for b in range(3):
+        hop0[b].wait()
+        for q in range(9 * b, 9 * b + 9):
+            psum[q] = (rsend[q, :, core].astype(F32) + rpair[q].astype(F32)).astype(BF)
+        for j in range(1, nx):
+            x = lax.rem(xme + j, nx)
+            src, dst = psum.at[pl.ds(9 * b, 9), x], rs1.at[xme, pl.ds(9 * b, 9)]
+            dev = (dp, 2 * x + core, tz)
+            hop1.append(remote(src, dst, r1s.at[b, j], r1r.at[b, nx - j], dev))
+            hop1[-1].start()
+
+    def turned(after, before):
+        return jnp.concatenate([after, before], 0).astype(F32).T.astype(BF)
+
+    def fill(dst, get_y, get_d, get_z):
+        r, c = iota((32, 256), 0), iota((32, 256), 1)
+
+        def place(row, ok):
+            after = (r == row) & (c == 127) & side[1] & ok
+            return one_hot(after | ((r == 16 + row) & (c == 128) & side[0] & ok))
+
         for s in (1, 0):
             ok = up[0] if s == 1 else up[1]
             mid = valid(ok, get_y(s))
-            after, before = valid(ok & side[1], get_d(s, 0)), valid(ok & side[0], get_d(s, 1))
-            out = mm(mid, shifts[0]) + mm(after, shifts[1]) + mm(before, shifts[2])
+            corner = turned(get_d(s, 0), get_d(s, 1))
+            corner = corner[96:128] if s == 1 else corner[0:32]
+            out = mm(mid, shifts[...]) + mm(corner, place(15 if s == 1 else 0, ok))
             rows, lanes = (slice(0, 32), slice(0, 128)) if s == 1 else (slice(1056, 1088), slice(128, 256))
             dst[0, rows, lanes] = mid
             dst[2, rows, lanes] = out[:, :128].astype(BF)
             dst[1, rows, lanes] = out[:, 128:].astype(BF)
-        r, c = iota((32, 256), 0), iota((32, 256), 1)
-        place = one_hot(
-            ((r == first) & (c == 127) & side[1]) | ((r == 17 + first) & (c == 128) & side[0])
-        )
+        edge = turned(get_z(0), get_z(1))
         for h in range(2):
             lanes = slice(128 * h, 128 * h + 128)
             for j in range(8):
                 rows = slice(32 + 128 * j, 160 + 128 * j)
-                got = slice((8 * h + j) * 16, (8 * h + j) * 16 + 16)
-                edge = jnp.concatenate([get_z(0, got), get_z(1, got)], 0)
-                out = mm(dst[0, rows, lanes], shifts[0]) + mm(edge, place, TN)
+                out = mm(dst[0, rows, lanes], shifts[...]) + mm(edge, place(8 * h + j, True))
                 dst[2, rows, lanes] = out[:, :128].astype(BF)
                 dst[1, rows, lanes] = out[:, 128:].astype(BF)
         for v in range(3):
@@ -308,13 +350,12 @@
             dst[v, 1056:1088, 0:128] = dst[v, 32:64, 128:256]
 
     for n, dst in enumerate((xin, xcot)):
-        rows = slice(32 * n, 32 * n + 32)
+        rows, tile = slice(32 * n, 32 * n + 32), slice(16 * n, 16 * n + 16)
         fill(
             dst,
-            2 * n,
             lambda s, rows=rows: yrecv[s, rows, :],
-            lambda s, t, rows=rows: drecv[s, t, rows, :],
-            lambda t, got: zrecv[t, got, :],
+            lambda s, t, tile=tile: drecv[s, t, tile, :],
+            lambda t, tile=tile: zrecv[t, tile, :],
         )
 
     version = (1, 0, 2)
@@ -340,23 +381,19 @@
 
     lax.fori_loop(0, 8, forward, 0)
 
-    for h in range(2):
-        lanes = slice(128 * h, 128 * h + 128)
-        edge = mm(pick(0), xdp[0, 32:1056, lanes], NT).astype(BF)
-        for j in range(8):
-            rows = slice((8 * h + j) * 16, (8 * h + j) * 16 + 16)
-            zsend2[rows, :] = edge[:, 128 * j : 128 * j + 128]
+    columns = extract(xdp)
+    zsend2[0] = columns[0:16]
+    zsend2[1] = columns[16:32]
     ysend2[0] = xdp[0, 32:64, 0:128]
     ysend2[1] = xdp[0, 1024:1056, 128:256]
     halo2 = []
     for s in range(2):
-        halo2.append(remote(ysend2.at[s], yrecv2.at[s, 0], gs.at[s], gr.at[s], at(step[s], 0)))
-        halo2.append(remote(zsend2, zrecv2.at[s], gs.at[2 + s], gr.at[2 + s], at(0, step[s])))
+        halo2.append(remote(ysend2.at[s], yrecv2.at[s], gs.at[s], gr.at[s], at(step[s], 0)))
+        halo2.append(remote(zsend2.at[s], zrecv2.at[s], gs.at[2 + s], gr.at[2 + s], at(0, step[s])))
         for t in range(2):
             q = 4 + 2 * s + t
-            halo2.append(
-                remote(ysend2.at[s], yrecv2.at[s, 1 + t], gs.at[q], gr.at[q], at(step[s], step[t]))
-            )
+            dev = at(step[s], step[t])
+            halo2.append(remote(zsend2.at[t], drecv2.at[s, t], gs.at[q], gr.at[q], dev))
     for copy in halo2:
         copy.start()
 
@@ -402,14 +439,15 @@
         copy.start()
     ar1[ty] = fpart[pl.ds(pl.multiple_of(ty * slab, 8), slab), :]
 
-    rs1[ty] = rsend[:, pl.ds(pl.multiple_of(ty * wide_o, 16), wide_o), :]
+    rs1[xme] = psum[:, xme]
     for copy in hop1:
         copy.wait()
 
-    def sum1(k, carry):
-        total = rs1[0, k].astype(F32)
-        for t in range(1, nty):
-            total = total + rs1[t, k].astype(F32)
+    def sum1(q, carry):
+        total = rs1[0, q].astype(F32)
+        for t in range(1, nx):
+            total = total + rs1[t, q].astype(F32)
+        k = 9 * (lax.div(q, 3) % 3) + 3 * lax.div(q, 9) + q % 3
         qf[pl.ds(k, wide_o, stride=32), :] = total
         return carry
 
@@ -440,6 +478,8 @@
         copy.start()
     ar2[me] = fsum1[...]
 
+    loads[6].wait()
+
     def coarse(q, carry):
         out = None
         for a in range(3):
@@ -469,10 +509,9 @@
         copy.wait()
     fill(
         xdp,
-        0,
-        lambda s: yrecv2[s, 0],
-        lambda s, t: yrecv2[s, 1 + t],
-        lambda t, got: zrecv2[t, got, :],
+        lambda s: yrecv2[s],
+        lambda s, t: drecv2[s, t],
+        lambda t: zrecv2[t],
     )
 
     def last(j, carry):
@@ -519,17 +558,24 @@
     sizes = tuple(mesh.shape[a] for a in ("dp", "ty", "tz"))
     ndp, nty, ntz = sizes
     zgroup = ndp * ntz
-    wide_o = 128 // nty
+    wide_o, nx = 128 // nty, nty // 2
     slab = 192 // nty
 
     def per_device(fine_input, fine_cotangent, first_weight, second_weight, coarse_input, coarse_cotangent, coarse_weight):
-        def turned(w):
-            return w[::-1].transpose(0, 2, 1).reshape(432, 16)
+        def by_offset(w):
+            return w.transpose(1, 2, 0).reshape(256, 27)
 
         dma = pltpu.SemaphoreType.DMA
         scratch = [
+            pltpu.VMEM((32, 64, 128), BF),
+            pltpu.VMEM((32, 64, 128), BF),
+            pltpu.VMEM((256, 27), BF),
+            pltpu.VMEM((256, 27), BF),
+            pltpu.VMEM((1024, 128), BF),
+            pltpu.VMEM((1024, 128), BF),
+            pltpu.VMEM((3456, 128), BF),
             pltpu.VMEM((512, 512), BF),
-            pltpu.VMEM((3, 128, 256), BF),
+            pltpu.VMEM((128, 256), BF),
             pltpu.VMEM((3, ROWS, 256), BF),
             pltpu.VMEM((3, ROWS, 256), BF),
             pltpu.VMEM((3, ROWS, 256), BF),
@@ -537,21 +583,24 @@
             pltpu.VMEM((3, 3, 128, 256), BF),
             pltpu.VMEM((2, 192, 128), BF),
             pltpu.VMEM((2, 192, 128), BF),
-            pltpu.VMEM((2, 384, 128), BF),
-            pltpu.VMEM((2, 384, 128), BF),
-            pltpu.VMEM((2, 2, 80, 128), BF),
-            pltpu.VMEM((2, 2, 80, 128), BF),
+            pltpu.VMEM((2, 160, 128), BF),
+            pltpu.VMEM((2, 160, 128), BF),
+            pltpu.VMEM((2, 2, 48, 128), BF),
+            pltpu.VMEM((2, 2, 48, 128), BF),
             pltpu.VMEM((2, 32, 128), BF),
-            pltpu.VMEM((2, 3, 32, 128), BF),
-            pltpu.VMEM((256, 128), BF),
-            pltpu.VMEM((2, 256, 128), BF),
+            pltpu.VMEM((2, 32, 128), BF),
+            pltpu.VMEM((2, 16, 128), BF),
+            pltpu.VMEM((2, 16, 128), BF),
+            pltpu.VMEM((2, 2, 16, 128), BF),
             pltpu.VMEM((1280, 128), F32),
             pltpu.VMEM((1280, 128), F32),
             pltpu.VMEM((1280, 128), F32),
             pltpu.VMEM((18, 64, 1152), BF),
             pltpu.VMEM((1152, 384), BF),
-            pltpu.VMEM((27, 128, 128), BF),
-            pltpu.VMEM((nty, 27, wide_o, 128), BF),
+            pltpu.VMEM((27, nx, 2, wide_o, 128), BF),
+            pltpu.VMEM((27, nx, wide_o, 128), BF),
+            pltpu.VMEM((27, nx, wide_o, 128), BF),
+            pltpu.VMEM((nx, 27, wide_o, 128), BF),
             pltpu.VMEM((32 * wide_o, 128), F32),
             pltpu.VMEM((32 * wide_o, 128), BF),
             pltpu.VMEM((zgroup, 32 * wide_o // ntz, 128), BF),
@@ -563,12 +612,15 @@
             pltpu.VMEM((zgroup, slab, 128), F32),
             pltpu.VMEM((slab, 128), F32),
             pltpu.VMEM((nty, slab, 128), F32),
+            dma((7,)),
             dma((8,)),
             dma((8,)),
+            dma((3,)),
+            dma((3,)),
             dma((8,)),
             dma((8,)),
-            dma((nty,)),
-            dma((nty,)),
+            dma((3, nx)),
+            dma((3, nx)),
             dma((zgroup,)),
             dma((zgroup,)),
             dma((nty,)),
@@ -588,7 +640,7 @@
                 jax.ShapeDtypeStruct((1024, 128), BF),
                 jax.ShapeDtypeStruct((wide_o // ntz, 27, 128), F32),
             ),
-            in_specs=[vmem] * 8,
+            in_specs=[pl.BlockSpec(memory_space=pltpu.HBM)] * 7,
             out_specs=(vmem,) * 5,
             scratch_shapes=scratch,
             compiler_params=pltpu.CompilerParams(
@@ -597,9 +649,8 @@
         )(
             fine_input.reshape(32, 64, 128),
             fine_cotangent.reshape(32, 64, 128),
-            first_weight.reshape(432, 16),
-            turned(first_weight),
-            turned(second_weight),
+            by_offset(first_weight),
+            by_offset(second_weight),
             coarse_input.reshape(1024, 128),
             coarse_cotangent.reshape(1024, 128),
             coarse_weight.reshape(3456, 128),

time: 55.7 us -> 52.3 us (0.939)
  Pallas kernels: 44.3 us -> 40.6 us
    pallas_call x1, Pallas kernels: 44.3 us -> 40.6 us  [per_device(): pl.pallas_call(functools.partial(kernel, sizes), out_shape=(jax.ShapeDtyp...]
    unnamed x16 -> x19, local copies, waits for them, and re-layouts: 7.99 us -> 10.6 us
    rev x2 -> x0, local copies, waits for them, and re-layouts: 1.97 us -> none  [turned(): return w[::-1].transpose(0, 2, 1).reshape(432, 16)]
where the time goes in v2:
time: 52.3 us; the launch traced here: 51.9 us
  Pallas kernels  40.6 us (78%)
  local copies, waits for them, and re-layouts  10.6 us (20%)
  between operations  0.66 us (1%)
    pallas_call x1, Pallas kernels, per_device(): pl.pallas_call(functools.partial(kernel, sizes), out_shape=(jax.ShapeDtyp...  40.6 us
    unnamed x19, local copies, waits for them, and re-layouts  10.6 us

profile of v2, /device:TPU:1, one launch (start us, length us, event | category | flops | bytes accessed | tf_op | source)
XLA Modules:
  0.0 51.9 jit_solution(9135129325926145415)
XLA Ops:
  0.6 0.0 copy-start
  0.6 1.2 %copy-done = bf16[27,128,128]{2,1,0:T(8,128)(2,1)S(1)} copy-done((bf16[27,128,128]{2,1,0:T(8,128)(2,1)S(1)}, bf16[27,128,128]{2,1,0:T(8,128)(2,1)}, u32[]{:S(2)}) %copy-start) | copy-done | bytes 884760
  1.8 0.0 copy-start.1
  1.8 1.0 %copy-done.1 = bf16[1,16,2,64,128]{4,3,2,1,0:T(8,128)(2,1)S(1)} copy-done((bf16[1,16,2,64,128]{4,3,2,1,0:T(8,128)(2,1)S(1)}, bf16[1,16,2,64,128]{4,3,2,1,0:T(8,128)(2,1)}, u32[]{:S(2)}) %copy-start.1) | copy-done | bytes 524312
  2.8 0.0 copy-start.2
  2.8 1.0 %copy-done.2 = bf16[1,16,2,64,128]{4,3,2,1,0:T(8,128)(2,1)S(1)} copy-done((bf16[1,16,2,64,128]{4,3,2,1,0:T(8,128)(2,1)S(1)}, bf16[1,16,2,64,128]{4,3,2,1,0:T(8,128)(2,1)}, u32[]{:S(2)}) %copy-start.2) | copy-done | bytes 524312
  3.9 0.0 copy-start.3
  3.9 0.9 %copy-done.3 = bf16[1,16,8,8,128]{4,3,2,1,0:T(8,128)(2,1)S(1)} copy-done((bf16[1,16,8,8,128]{4,3,2,1,0:T(8,128)(2,1)S(1)}, bf16[1,16,8,8,128]{4,3,2,1,0:T(8,128)(2,1)}, u32[]{:S(2)}) %copy-start.3) | copy-done | bytes 262168
  4.8 0.0 copy-start.4
  4.8 0.9 %copy-done.4 = bf16[1,16,8,8,128]{4,3,2,1,0:T(8,128)(2,1)S(1)} copy-done((bf16[1,16,8,8,128]{4,3,2,1,0:T(8,128)(2,1)S(1)}, bf16[1,16,8,8,128]{4,3,2,1,0:T(8,128)(2,1)}, u32[]{:S(2)}) %copy-start.4) | copy-done | bytes 262168
  5.8 0.0 copy-start.5
  5.8 0.8 %copy-done.5 = bf16[27,16,16]{0,2,1:T(8,128)(2,1)S(1)} copy-done((bf16[27,16,16]{0,2,1:T(8,128)(2,1)S(1)}, bf16[27,16,16]{0,2,1:T(8,128)(2,1)}, u32[]{:S(2)}) %copy-start.5) | copy-done | bytes 13848
  6.6 0.0 copy-start.6
  6.6 0.8 %copy-done.6 = bf16[27,16,16]{0,2,1:T(8,128)(2,1)S(1)} copy-done((bf16[27,16,16]{0,2,1:T(8,128)(2,1)S(1)}, bf16[27,16,16]{0,2,1:T(8,128)(2,1)}, u32[]{:S(2)}) %copy-start.6) | copy-done | bytes 13848
  7.5 40.6 %shard_map.110 = (bf16[32,64,128]{2,1,0:T(8,128)(2,1)S(1)}, f32[27,16,16]{2,1,0:T(8,128)S(1)}, f32[27,16,16]{2,1,0:T(8,128)S(1)}, bf16[1024,128]{1,0:T(8,128)(2,1)S(1)}, f32[2,27,128]{2,1,0:T(8,128)S(1)}) custom-call(bf16[32,64,128]{2,1,0:T(8,128)(2,1)S(1)} %bitcast.14, bf16[32,64,128]{2,1,0:T(8,128)(2,1)S(1)} %bitcast.15, bf16[256,27]{1,0:T(8,128)(2,1)S(1)} %bitcast.20, ...), custom_call_target="tpu_custom_call" | custom-call | tf_op jit(solution)/shard_map/pallas_call | solution.py:634
  48.1 0.6 %copy.14 = f32[2,27,128]{2,0,1:T(2,128)} copy(f32[2,27,128]{2,1,0:T(8,128)S(1)} %get-tuple-element.19) | data formatting | bytes 55296
  48.7 0.8 %copy.12 = f32[27,16,16]{0,2,1:T(8,128)} copy(f32[27,16,16]{2,1,0:T(8,128)S(1)} %get-tuple-element.16) | data formatting | bytes 55296
  49.5 0.8 %copy.13 = f32[27,16,16]{0,2,1:T(8,128)} copy(f32[27,16,16]{2,1,0:T(8,128)S(1)} %get-tuple-element.17) | data formatting | bytes 55296
  50.4 0.8 %copy.17 = bf16[1,16,2,64,128]{4,3,2,1,0:T(8,128)(2,1)} copy(bf16[1,16,2,64,128]{4,3,2,1,0:T(8,128)(2,1)S(1)} %bitcast.16) | data formatting | bytes 1048576
  51.2 0.7 %copy.18 = bf16[1,16,8,8,128]{4,3,2,1,0:T(8,128)(2,1)} copy(bf16[1,16,8,8,128]{4,3,2,1,0:T(8,128)(2,1)S(1)} %bitcast.19) | data formatting | bytes 524288
Async XLA Ops:
  0.6 1.2 %copy-start = (bf16[27,128,128]{2,1,0:T(8,128)(2,1)S(1)}, bf16[27,128,128]{2,1,0:T(8,128)(2,1)}, u32[]{:S(2)}) copy-start(bf16[27,128,128]{2,1,0:T(8,128)(2,1)} %param.13) | copy-start | bytes 2654212
  1.8 1.0 %copy-start.1 = (bf16[1,16,2,64,128]{4,3,2,1,0:T(8,128)(2,1)S(1)}, bf16[1,16,2,64,128]{4,3,2,1,0:T(8,128)(2,1)}, u32[]{:S(2)}) copy-start(bf16[1,16,2,64,128]{4,3,2,1,0:T(8,128)(2,1)} %param.7) | copy-start | bytes 1572868
  2.8 1.0 %copy-start.2 = (bf16[1,16,2,64,128]{4,3,2,1,0:T(8,128)(2,1)S(1)}, bf16[1,16,2,64,128]{4,3,2,1,0:T(8,128)(2,1)}, u32[]{:S(2)}) copy-start(bf16[1,16,2,64,128]{4,3,2,1,0:T(8,128)(2,1)} %param.8) | copy-start | bytes 1572868
  3.9 0.9 %copy-start.3 = (bf16[1,16,8,8,128]{4,3,2,1,0:T(8,128)(2,1)S(1)}, bf16[1,16,8,8,128]{4,3,2,1,0:T(8,128)(2,1)}, u32[]{:S(2)}) copy-start(bf16[1,16,8,8,128]{4,3,2,1,0:T(8,128)(2,1)} %param.11) | copy-start | bytes 786436
  4.8 0.9 %copy-start.4 = (bf16[1,16,8,8,128]{4,3,2,1,0:T(8,128)(2,1)S(1)}, bf16[1,16,8,8,128]{4,3,2,1,0:T(8,128)(2,1)}, u32[]{:S(2)}) copy-start(bf16[1,16,8,8,128]{4,3,2,1,0:T(8,128)(2,1)} %param.12) | copy-start | bytes 786436
  5.8 0.8 %copy-start.5 = (bf16[27,16,16]{0,2,1:T(8,128)(2,1)S(1)}, bf16[27,16,16]{0,2,1:T(8,128)(2,1)}, u32[]{:S(2)}) copy-start(bf16[27,16,16]{0,2,1:T(8,128)(2,1)} %param.9) | copy-start | bytes 41476
  6.6 0.8 %copy-start.6 = (bf16[27,16,16]{0,2,1:T(8,128)(2,1)S(1)}, bf16[27,16,16]{0,2,1:T(8,128)(2,1)}, u32[]{:S(2)}) copy-start(bf16[27,16,16]{0,2,1:T(8,128)(2,1)} %param.10) | copy-start | bytes 41476

commit v3 on v2

--- a/solution.py
+++ b/solution.py
@@ -530,7 +530,7 @@
     for t in range(1, zgroup):
         total = total + rs2[t].astype(F32)
     for o in range(wide_o // ntz):
-        o_gc[o] = total[32 * o : 32 * o + 27, :]
+        o_gc[:, o, :] = total[32 * o : 32 * o + 27, :]
 
     for copy in hop_c:
         copy.wait()
@@ -552,6 +552,20 @@
                     two = part if two is None else two + part
                 o_gf[k] = one
                 o_gs[26 - k] = two
+
+
+def finish(gfi, gf, gs, gci, gc, o_gfi, o_gf, o_gs, o_gci, o_gc, sems):
+    copies = [
+        pltpu.make_async_copy(src, dst, sems.at[n])
+        for n, (src, dst) in enumerate(((gfi, o_gfi), (gci, o_gci), (gc, o_gc)))
+    ]
+    for copy in copies:
+        copy.start()
+    for src, dst in ((gf, o_gf), (gs, o_gs)):
+        for o in range(16):
+            dst[o] = src[:, o, :].T
+    for copy in copies:
+        copy.wait()
 
 
 def solution(mesh):
@@ -638,13 +652,13 @@
                 jax.ShapeDtypeStruct((27, 16, 16), F32),
                 jax.ShapeDtypeStruct((27, 16, 16), F32),
                 jax.ShapeDtypeStruct((1024, 128), BF),
-                jax.ShapeDtypeStruct((wide_o // ntz, 27, 128), F32),
+                jax.ShapeDtypeStruct((27, wide_o // ntz, 128), F32),
             ),
-            in_specs=[pl.BlockSpec(memory_space=pltpu.HBM)] * 7,
+            in_specs=[pl.BlockSpec(memory_space=pl.ANY)] * 7,
             out_specs=(vmem,) * 5,
             scratch_shapes=scratch,
             compiler_params=pltpu.CompilerParams(
-                collective_id=0, has_side_effects=True, vmem_limit_bytes=48 * 1024 * 1024
+                collective_id=0, has_side_effects=True, vmem_limit_bytes=60 * 1024 * 1024
             ),
         )(
             fine_input.reshape(32, 64, 128),
@@ -655,12 +669,27 @@
             coarse_cotangent.reshape(1024, 128),
             coarse_weight.reshape(3456, 128),
         )
+        far = pl.BlockSpec(memory_space=pl.ANY)
+        outs = pl.pallas_call(
+            finish,
+            out_shape=(
+                jax.ShapeDtypeStruct((32, 64, 128), BF),
+                jax.ShapeDtypeStruct((16, 16, 27), F32),
+                jax.ShapeDtypeStruct((16, 16, 27), F32),
+                jax.ShapeDtypeStruct((1024, 128), BF),
+                jax.ShapeDtypeStruct((27, wide_o // ntz, 128), F32),
+            ),
+            in_specs=[far, vmem, vmem, far, far],
+            out_specs=(far, vmem, vmem, far, far),
+            scratch_shapes=[dma((3,))],
+            compiler_params=pltpu.CompilerParams(vmem_limit_bytes=60 * 1024 * 1024),
+        )(*outs)
         return (
             outs[0].reshape(fine_input.shape),
-            outs[1],
-            outs[2],
+            outs[1].transpose(2, 0, 1),
+            outs[2].transpose(2, 0, 1),
             outs[3].reshape(coarse_input.shape),
-            outs[4],
+            outs[4].transpose(1, 0, 2),
         )
 
     fine = P("dp", None, None, "ty", "tz")

time: 52.3 us -> 69.4 us (1.33)
  Pallas kernels: 40.6 us -> 68.6 us
  local copies, waits for them, and re-layouts: 10.6 us -> 0 us
    pallas_call x0 -> x1, Pallas kernels: none -> 27.5 us  [per_device(): pl.pallas_call(finish, out_shape=(jax.ShapeDtypeStruct((32, 64, 128), BF)...]
    unnamed x19 -> x0, local copies, waits for them, and re-layouts: 10.6 us -> none
where the time goes in v3:
time: 69.4 us; the launch traced here: 69.2 us
  Pallas kernels  68.6 us (99%)
    pallas_call x1, Pallas kernels, per_device(): pl.pallas_call(functools.partial(kernel, sizes), out_shape=(jax.ShapeDtyp...  41 us
    pallas_call x1, Pallas kernels, per_device(): pl.pallas_call(finish, out_shape=(jax.ShapeDtypeStruct((32, 64, 128), BF)...  27.5 us

profile of v3, /device:TPU:1, one launch (start us, length us, event | category | flops | bytes accessed | tf_op | source)
XLA Modules:
  0.0 69.2 jit_solution(15707389420131611534)
XLA Ops:
  0.6 41.0 %shard_map.110 = (bf16[32,64,128]{2,1,0:T(8,128)(2,1)}, f32[27,16,16]{2,1,0:T(8,128)}, f32[27,16,16]{2,1,0:T(8,128)}, bf16[1024,128]{1,0:T(8,128)(2,1)}, f32[27,2,128]{2,1,0:T(2,128)}) custom-call(bf16[32,64,128]{2,1,0:T(8,128)(2,1)} %bitcast.17, bf16[32,64,128]{2,1,0:T(8,128)(2,1)} %bitcast.18, bf16[256,27]{1,0:T(8,128)(2,1)} %bitcast.21, ...), custom_call_target="tpu_custom_call" | custom-call | tf_op jit(solution)/shard_map/pallas_call | solution.py:648
  41.7 27.5 %shard_map.111 = (bf16[32,64,128]{2,1,0:T(8,128)(2,1)}, f32[16,16,27]{2,1,0:T(8,128)}, f32[16,16,27]{2,1,0:T(8,128)}, bf16[1024,128]{1,0:T(8,128)(2,1)}, f32[27,2,128]{2,1,0:T(2,128)}) custom-call(bf16[32,64,128]{2,1,0:T(8,128)(2,1)} %get-tuple-element.15.gfi, f32[27,16,16]{2,1,0:T(8,128)} %get-tuple-element.16.gf, f32[27,16,16]{2,1,0:T(8,128)} %get-tuple-element.17.gs, ...), custom_call_target="tpu_custom_call" | custom-call | tf_op jit(solution)/shard_map/pallas_call | solution.py:673

commit v4 on v3

--- a/solution.py
+++ b/solution.py
@@ -554,17 +554,19 @@
                 o_gs[26 - k] = two
 
 
-def finish(gfi, gf, gs, gci, gc, o_gfi, o_gf, o_gs, o_gci, o_gc, sems):
-    copies = [
-        pltpu.make_async_copy(src, dst, sems.at[n])
-        for n, (src, dst) in enumerate(((gfi, o_gfi), (gci, o_gci), (gc, o_gc)))
-    ]
-    for copy in copies:
+def finish(gfi, gf, gs, gci, gc, o_gfi, o_gf, o_gs, o_gci, o_gc, v_gfi, v_gci, v_gc, sems):
+    moves = ((gfi, v_gfi, o_gfi), (gci, v_gci, o_gci), (gc, v_gc, o_gc))
+    into = [pltpu.make_async_copy(src, mid, sems.at[n]) for n, (src, mid, _) in enumerate(moves)]
+    out = [pltpu.make_async_copy(mid, dst, sems.at[3 + n]) for n, (_, mid, dst) in enumerate(moves)]
+    for copy in into:
         copy.start()
+    for n in range(3):
+        into[n].wait()
+        out[n].start()
     for src, dst in ((gf, o_gf), (gs, o_gs)):
         for o in range(16):
             dst[o] = src[:, o, :].T
-    for copy in copies:
+    for copy in out:
         copy.wait()
 
 
@@ -681,7 +683,12 @@
             ),
             in_specs=[far, vmem, vmem, far, far],
             out_specs=(far, vmem, vmem, far, far),
-            scratch_shapes=[dma((3,))],
+            scratch_shapes=[
+                pltpu.VMEM((32, 64, 128), BF),
+                pltpu.VMEM((1024, 128), BF),
+                pltpu.VMEM((27, wide_o // ntz, 128), F32),
+                dma((6,)),
+            ],
             compiler_params=pltpu.CompilerParams(vmem_limit_bytes=60 * 1024 * 1024),
         )(*outs)
         return (

time: 69.4 us -> 45.6 us (0.66)
  Pallas kernels: 68.6 us -> 44.8 us
    pallas_call x1, Pallas kernels: 27.5 us -> 3.71 us  [per_device(): pl.pallas_call(finish, out_shape=(jax.ShapeDtypeStruct((32, 64, 128), BF)...]
where the time goes in v4:
time: 45.6 us; the launch traced here: 45.4 us
  Pallas kernels  44.8 us (98%)
  between operations  0.64 us (1%)
    pallas_call x1, Pallas kernels, per_device(): pl.pallas_call(functools.partial(kernel, sizes), out_shape=(jax.ShapeDtyp...  41 us
    pallas_call x1, Pallas kernels, per_device(): pl.pallas_call(finish, out_shape=(jax.ShapeDtypeStruct((32, 64, 128), BF)...  3.71 us

profile of v4, /device:TPU:1, one launch (start us, length us, event | category | flops | bytes accessed | tf_op | source)
XLA Modules:
  0.0 45.4 jit_solution(6357644533607659197)
XLA Ops:
  0.6 41.0 %shard_map.110 = (bf16[32,64,128]{2,1,0:T(8,128)(2,1)}, f32[27,16,16]{2,1,0:T(8,128)}, f32[27,16,16]{2,1,0:T(8,128)}, bf16[1024,128]{1,0:T(8,128)(2,1)}, f32[27,2,128]{2,1,0:T(2,128)}) custom-call(bf16[32,64,128]{2,1,0:T(8,128)(2,1)} %bitcast.17, bf16[32,64,128]{2,1,0:T(8,128)(2,1)} %bitcast.18, bf16[256,27]{1,0:T(8,128)(2,1)} %bitcast.21, ...), custom_call_target="tpu_custom_call" | custom-call | tf_op jit(solution)/shard_map/pallas_call | solution.py:650
  41.7 3.7 %shard_map.111 = (bf16[32,64,128]{2,1,0:T(8,128)(2,1)}, f32[16,16,27]{2,1,0:T(8,128)}, f32[16,16,27]{2,1,0:T(8,128)}, bf16[1024,128]{1,0:T(8,128)(2,1)}, f32[27,2,128]{2,1,0:T(2,128)}) custom-call(bf16[32,64,128]{2,1,0:T(8,128)(2,1)} %get-tuple-element.15.gfi, f32[27,16,16]{2,1,0:T(8,128)} %get-tuple-element.16.gf, f32[27,16,16]{2,1,0:T(8,128)} %get-tuple-element.17.gs, ...), custom_call_target="tpu_custom_call" | custom-call | tf_op jit(solution)/shard_map/pallas_call | solution.py:675

commit v5 on v4

--- a/solution.py
+++ b/solution.py
@@ -62,8 +62,13 @@
     yrecv,
     zsend,
     zrecv,
-    dsend,
     drecv,
+    ycs,
+    ycr,
+    zcs,
+    zcr,
+    dcs,
+    dcr,
     ysend2,
     yrecv2,
     zsend2,
@@ -81,6 +86,13 @@
     qf,
     qb,
     rs2,
+    g_gci,
+    g_gfi,
+    g_gf,
+    g_gs,
+    t_gf,
+    t_gs,
+    g_gc,
     acc1,
     acc2,
     fpart,
@@ -92,6 +104,8 @@
     ls,
     hs,
     hr,
+    cs,
+    cr,
     ps,
     pr,
     gs,
@@ -106,6 +120,7 @@
     a2r,
     a3s,
     a3r,
+    ws,
 ):
     ndp, nty, ntz = sizes
     dp, ty, tz = lax.axis_index("dp"), lax.axis_index("ty"), lax.axis_index("tz")
@@ -180,8 +195,6 @@
         for t in range(2):
             tile = columns[16 * t : 16 * t + 16, :]
             zsend[t, 16 * n : 16 * n + 16, :] = tile
-            for q in range(2):
-                dsend[q, t, 16 * n : 16 * n + 16, :] = tile
 
     loads[0].wait()
     for x in range(16):
@@ -191,8 +204,8 @@
         return cflat[pl.ds(8 * y + z, 16, stride=80), :]
 
     for y in range(8):
-        zsend[0, 32 + 16 * y : 48 + 16 * y, :] = column(y + 1, 0).astype(BF)
-        zsend[1, 32 + 16 * y : 48 + 16 * y, :] = column(y + 1, 7).astype(BF)
+        zcs[0, 16 * y : 16 * y + 16, :] = column(y + 1, 0).astype(BF)
+        zcs[1, 16 * y : 16 * y + 16, :] = column(y + 1, 7).astype(BF)
     for s in range(2):
         own = (slice(32, 64), slice(0, 128)) if s == 0 else (slice(1024, 1056), slice(128, 256))
         ysend[s, 0:32, :] = xin[(0, *own)]
@@ -200,23 +213,25 @@
         first = 8 if s == 0 else 64
         for x in range(0, 16, 2):
             pair = [cflat[80 * (x + q) + first : 80 * (x + q) + first + 8, :] for q in range(2)]
-            ysend[s, 64 + 8 * x : 80 + 8 * x, :] = jnp.concatenate(pair, 0).astype(BF)
+            ycs[s, 8 * x : 8 * x + 16, :] = jnp.concatenate(pair, 0).astype(BF)
         for t in range(2):
-            dsend[s, t, 32:48, :] = column(1 if s == 0 else 8, 0 if t == 0 else 7).astype(BF)
+            dcs[s, t] = column(1 if s == 0 else 8, 0 if t == 0 else 7).astype(BF)
 
     pl.semaphore_wait(barrier, len(partners))
 
     step = (-1, 1)
-    halo = []
+    halo, halo_c = [], []
     for s in range(2):
-        halo.append(remote(ysend.at[s], yrecv.at[s], hs.at[s], hr.at[s], at(step[s], 0)))
-        halo.append(remote(zsend.at[s], zrecv.at[s], hs.at[2 + s], hr.at[2 + s], at(0, step[s])))
         for t in range(2):
-            q = 4 + 2 * s + t
-            halo.append(
-                remote(dsend.at[s, t], drecv.at[s, t], hs.at[q], hr.at[q], at(step[s], step[t]))
-            )
-    for copy in halo:
+            q, dev = 4 + 2 * s + t, at(step[s], step[t])
+            halo.append(remote(zsend.at[t], drecv.at[s, t], hs.at[q], hr.at[q], dev))
+            halo_c.append(remote(dcs.at[s, t], dcr.at[s, t], cs.at[q], cr.at[q], dev))
+        y, z, q = at(step[s], 0), at(0, step[s]), 2 + s
+        halo.append(remote(zsend.at[s], zrecv.at[s], hs.at[q], hr.at[q], z))
+        halo.append(remote(ysend.at[s], yrecv.at[s], hs.at[s], hr.at[s], y))
+        halo_c.append(remote(zcs.at[s], zcr.at[s], cs.at[q], cr.at[q], z))
+        halo_c.append(remote(ycs.at[s], ycr.at[s], cs.at[s], cr.at[s], y))
+    for copy in halo + halo_c:
         copy.start()
 
     lane = iota((32, 768), 1)
@@ -258,64 +273,11 @@
     vmat[17] = jnp.zeros((64, 1152), BF)
     qf[...] = jnp.zeros_like(qf)
 
-    for copy in halo:
-        copy.wait()
-
     def valid(cond, value):
         return jnp.where(cond, value, jnp.zeros_like(value))
 
-    for x in range(16):
-        rows = slice(64 + 8 * (x // 2 * 2), 80 + 8 * (x // 2 * 2))
-        half = slice(8 * (x % 2), 8 * (x % 2) + 8)
-        cflat[80 * x : 80 * x + 8, :] = valid(up[0], yrecv[1, rows, :].astype(F32)[half])
-        cflat[80 * x + 72 : 80 * x + 80, :] = valid(up[1], yrecv[0, rows, :].astype(F32)[half])
-    cplus[...] = pltpu.roll(cflat[...], 1279, 0)
-    cminus[...] = pltpu.roll(cflat[...], 1, 0)
-    for y in range(10):
-        for ref, z, t, ok in ((cplus, 7, 0, side[1]), (cminus, 0, 1, side[0])):
-            if y == 0:
-                part, ok = drecv[1, t, 32:48, :], ok & up[0]
-            elif y == 9:
-                part, ok = drecv[0, t, 32:48, :], ok & up[1]
-            else:
-                part = zrecv[t, 32 + 16 * (y - 1) : 48 + 16 * (y - 1), :]
-            ref[pl.ds(8 * y + z, 16, stride=80), :] = valid(ok, part.astype(F32))
-
-    def spread(x, carry):
-        for b in range(3):
-            for cc, ref in enumerate((cplus, cflat, cminus)):
-                rows = ref[pl.ds(pl.multiple_of(x * 80 + 8 * (2 - b), 8), 64), :]
-                q = 3 * b + cc
-                vmat[x + 1, :, 128 * q : 128 * q + 128] = rows.astype(BF)
-        return carry
-
-    lax.fori_loop(0, 16, spread, 0)
-
-    wide_o, nx = 128 // nty, nty // 2
-    core, xme = lax.rem(ty, 2), lax.div(ty, 2)
-    other = (dp, ty + 1 - 2 * core, tz)
-    hop0 = []
-    for b in range(3):
-        left = vmat[:, :, 384 * b : 384 * b + 384].reshape(1152, 384)
-        g = mm(left, inp3[...], TN)
-        for a in range(3):
-            for cc in range(3):
-                part = g[128 * cc : 128 * cc + 128, 128 * a : 128 * a + 128]
-                rsend[9 * b + 3 * a + cc] = part.astype(BF).reshape(nx, 2, wide_o, 128)
-        src = rsend.at[pl.ds(9 * b, 9), :, 1 - core]
-        hop0.append(remote(src, rpair.at[pl.ds(9 * b, 9)], ps.at[b], pr.at[b], other))
-        hop0[b].start()
-    hop1 = []
-    for b in range(3):
-        hop0[b].wait()
-        for q in range(9 * b, 9 * b + 9):
-            psum[q] = (rsend[q, :, core].astype(F32) + rpair[q].astype(F32)).astype(BF)
-        for j in range(1, nx):
-            x = lax.rem(xme + j, nx)
-            src, dst = psum.at[pl.ds(9 * b, 9), x], rs1.at[xme, pl.ds(9 * b, 9)]
-            dev = (dp, 2 * x + core, tz)
-            hop1.append(remote(src, dst, r1s.at[b, j], r1r.at[b, nx - j], dev))
-            hop1[-1].start()
+    for copy in halo:
+        copy.wait()
 
     def turned(after, before):
         return jnp.concatenate([after, before], 0).astype(F32).T.astype(BF)
@@ -397,6 +359,50 @@
     for copy in halo2:
         copy.start()
 
+    for copy in halo_c:
+        copy.wait()
+    for x in range(16):
+        rows = slice(8 * (x // 2 * 2), 16 + 8 * (x // 2 * 2))
+        half = slice(8 * (x % 2), 8 * (x % 2) + 8)
+        cflat[80 * x : 80 * x + 8, :] = valid(up[0], ycr[1, rows, :].astype(F32)[half])
+        cflat[80 * x + 72 : 80 * x + 80, :] = valid(up[1], ycr[0, rows, :].astype(F32)[half])
+    cplus[...] = pltpu.roll(cflat[...], 1279, 0)
+    cminus[...] = pltpu.roll(cflat[...], 1, 0)
+    for y in range(10):
+        for ref, z, t, ok in ((cplus, 7, 0, side[1]), (cminus, 0, 1, side[0])):
+            if y == 0:
+                part, ok = dcr[1, t], ok & up[0]
+            elif y == 9:
+                part, ok = dcr[0, t], ok & up[1]
+            else:
+                part = zcr[t, 16 * (y - 1) : 16 * y, :]
+            ref[pl.ds(8 * y + z, 16, stride=80), :] = valid(ok, part.astype(F32))
+
+    def spread(x, carry):
+        for b in range(3):
+            for cc, ref in enumerate((cplus, cflat, cminus)):
+                rows = ref[pl.ds(pl.multiple_of(x * 80 + 8 * (2 - b), 8), 64), :]
+                q = 3 * b + cc
+                vmat[x + 1, :, 128 * q : 128 * q + 128] = rows.astype(BF)
+        return carry
+
+    lax.fori_loop(0, 16, spread, 0)
+
+    wide_o, nx = 128 // nty, nty // 2
+    core, xme = lax.rem(ty, 2), lax.div(ty, 2)
+    other = (dp, ty + 1 - 2 * core, tz)
+    hop0 = []
+    for b in range(3):
+        left = vmat[:, :, 384 * b : 384 * b + 384].reshape(1152, 384)
+        g = mm(left, inp3[...], TN)
+        for a in range(3):
+            for cc in range(3):
+                part = g[128 * cc : 128 * cc + 128, 128 * a : 128 * a + 128]
+                rsend[9 * b + 3 * a + cc] = part.astype(BF).reshape(nx, 2, wide_o, 128)
+        src = rsend.at[pl.ds(9 * b, 9), :, 1 - core]
+        hop0.append(remote(src, rpair.at[pl.ds(9 * b, 9)], ps.at[b], pr.at[b], other))
+        hop0[b].start()
+
     acc1[...] = jnp.zeros_like(acc1)
     acc2[...] = jnp.zeros_like(acc2)
 
@@ -439,30 +445,32 @@
         copy.start()
     ar1[ty] = fpart[pl.ds(pl.multiple_of(ty * slab, 8), slab), :]
 
-    rs1[xme] = psum[:, xme]
-    for copy in hop1:
-        copy.wait()
-
-    def sum1(q, carry):
-        total = rs1[0, q].astype(F32)
-        for t in range(1, nx):
-            total = total + rs1[t, q].astype(F32)
-        k = 9 * (lax.div(q, 3) % 3) + 3 * lax.div(q, 9) + q % 3
-        qf[pl.ds(k, wide_o, stride=32), :] = total
+    hop1 = []
+    for b in range(3):
+        hop0[b].wait()
+        for q in range(9 * b, 9 * b + 9):
+            psum[q] = (rsend[q, :, core].astype(F32) + rpair[q].astype(F32)).astype(BF)
+        for j in range(1, nx):
+            x = lax.rem(xme + j, nx)
+            src, dst = psum.at[pl.ds(9 * b, 9), x], rs1.at[xme, pl.ds(9 * b, 9)]
+            dev = (dp, 2 * x + core, tz)
+            hop1.append(remote(src, dst, r1s.at[b, j], r1r.at[b, nx - j], dev))
+            hop1[-1].start()
+
+    loads[6].wait()
+
+    def coarse(q, carry):
+        out = None
+        for a in range(3):
+            left = vmat[pl.ds(q * 4 + 2 - a, 4)].reshape(256, 1152)
+            term = mm(left, wc[1152 * a : 1152 * a + 1152, :])
+            out = term if out is None else out + term
+        g_gci[pl.ds(pl.multiple_of(q * 256, 256), 256), :] = out.astype(BF)
         return carry
 
-    lax.fori_loop(0, 27, sum1, 0)
-    qb[...] = qf[...].astype(BF)
-    deep = 32 * wide_o // ntz
-
-    hop2 = []
-    for j in range(1, zgroup):
-        g, z, dev = z_peer(j)
-        src = qb.at[pl.ds(pl.multiple_of(z * deep, 16), deep), :]
-        hop2.append(remote(src, rs2.at[me], r2s.at[j], r2r.at[zgroup - j], dev))
-    for copy in hop2:
-        copy.start()
-    rs2[me] = qb[pl.ds(pl.multiple_of(tz * deep, 16), deep), :]
+    lax.fori_loop(0, 4, coarse, 0)
+    stores = [pltpu.make_async_copy(g_gci, o_gci, ws.at[0])]
+    stores[0].start()
 
     for copy in hop_a:
         copy.wait()
@@ -478,18 +486,26 @@
         copy.start()
     ar2[me] = fsum1[...]
 
-    loads[6].wait()
-
-    def coarse(q, carry):
-        out = None
-        for a in range(3):
-            left = vmat[pl.ds(q * 4 + 2 - a, 4)].reshape(256, 1152)
-            term = mm(left, wc[1152 * a : 1152 * a + 1152, :])
-            out = term if out is None else out + term
-        o_gci[pl.ds(pl.multiple_of(q * 256, 256), 256), :] = out.astype(BF)
+    for copy in halo2:
+        copy.wait()
+    fill(
+        xdp,
+        lambda s: yrecv2[s],
+        lambda s, t: drecv2[s, t],
+        lambda t: zrecv2[t],
+    )
+
+    def last(j, carry):
+        parts = [conv(2, xdp, 4 * j + q).astype(BF) for q in range(4)]
+        out = mm(perm[...], jnp.concatenate(parts, 0)).astype(BF)
+        first = pl.multiple_of(16 * j, 16)
+        g_gfi[:, pl.ds(first, 16), :] = out[:, :128].reshape(32, 16, 128)
+        g_gfi[:, pl.ds(first + 32, 16), :] = out[:, 128:].reshape(32, 16, 128)
         return carry
 
-    lax.fori_loop(0, 4, coarse, 0)
+    lax.fori_loop(0, 2, last, 0)
+    stores.append(pltpu.make_async_copy(g_gfi, o_gfi, ws.at[1]))
+    stores[1].start()
 
     for copy in hop_b:
         copy.wait()
@@ -505,32 +521,30 @@
         copy.start()
     gath[ty] = fsum2[...]
 
-    for copy in halo2:
-        copy.wait()
-    fill(
-        xdp,
-        lambda s: yrecv2[s],
-        lambda s, t: drecv2[s, t],
-        lambda t: zrecv2[t],
-    )
-
-    def last(j, carry):
-        parts = [conv(2, xdp, 4 * j + q).astype(BF) for q in range(4)]
-        out = mm(perm[...], jnp.concatenate(parts, 0)).astype(BF)
-        first = pl.multiple_of(16 * j, 16)
-        o_gfi[:, pl.ds(first, 16), :] = out[:, :128].reshape(32, 16, 128)
-        o_gfi[:, pl.ds(first + 32, 16), :] = out[:, 128:].reshape(32, 16, 128)
+    rs1[xme] = psum[:, xme]
+    for copy in hop1:
+        copy.wait()
+
+    def sum1(q, carry):
+        total = rs1[0, q].astype(F32)
+        for t in range(1, nx):
+            total = total + rs1[t, q].astype(F32)
+        k = 9 * (lax.div(q, 3) % 3) + 3 * lax.div(q, 9) + q % 3
+        qf[pl.ds(k, wide_o, stride=32), :] = total
         return carry
 
-    lax.fori_loop(0, 2, last, 0)
-
+    lax.fori_loop(0, 27, sum1, 0)
+    qb[...] = qf[...].astype(BF)
+    deep = 32 * wide_o // ntz
+
+    hop2 = []
+    for j in range(1, zgroup):
+        g, z, dev = z_peer(j)
+        src = qb.at[pl.ds(pl.multiple_of(z * deep, 16), deep), :]
+        hop2.append(remote(src, rs2.at[me], r2s.at[j], r2r.at[zgroup - j], dev))
     for copy in hop2:
-        copy.wait()
-    total = rs2[0].astype(F32)
-    for t in range(1, zgroup):
-        total = total + rs2[t].astype(F32)
-    for o in range(wide_o // ntz):
-        o_gc[:, o, :] = total[32 * o : 32 * o + 27, :]
+        copy.start()
+    rs2[me] = qb[pl.ds(pl.multiple_of(tz * deep, 16), deep), :]
 
     for copy in hop_c:
         copy.wait()
@@ -550,22 +564,36 @@
                     lanes = slice(32 * cc + 16 * xo, 32 * cc + 16 * xo + 16)
                     part = fpart[first : first + 16, lanes]
                     two = part if two is None else two + part
-                o_gf[k] = one
-                o_gs[26 - k] = two
-
-
-def finish(gfi, gf, gs, gci, gc, o_gfi, o_gf, o_gs, o_gci, o_gc, v_gfi, v_gci, v_gc, sems):
-    moves = ((gfi, v_gfi, o_gfi), (gci, v_gci, o_gci), (gc, v_gc, o_gc))
-    into = [pltpu.make_async_copy(src, mid, sems.at[n]) for n, (src, mid, _) in enumerate(moves)]
-    out = [pltpu.make_async_copy(mid, dst, sems.at[3 + n]) for n, (_, mid, dst) in enumerate(moves)]
+                g_gf[k] = one
+                g_gs[26 - k] = two
+    for n, (src, mid, dst) in enumerate(((g_gf, t_gf, o_gf), (g_gs, t_gs, o_gs))):
+        for o in range(16):
+            mid[o] = src[:, o, :].T
+        stores.append(pltpu.make_async_copy(mid, dst, ws.at[2 + n]))
+        stores[2 + n].start()
+
+    for copy in hop2:
+        copy.wait()
+    total = rs2[0].astype(F32)
+    for t in range(1, zgroup):
+        total = total + rs2[t].astype(F32)
+    for o in range(wide_o // ntz):
+        g_gc[:, o, :] = total[32 * o : 32 * o + 27, :]
+    stores.append(pltpu.make_async_copy(g_gc, o_gc, ws.at[4]))
+    stores[4].start()
+    for copy in stores:
+        copy.wait()
+
+
+def finish(*refs):
+    srcs, dsts, mids, sems = refs[:5], refs[5:10], refs[10:15], refs[15]
+    into = [pltpu.make_async_copy(srcs[n], mids[n], sems.at[n]) for n in range(5)]
+    out = [pltpu.make_async_copy(mids[n], dsts[n], sems.at[5 + n]) for n in range(5)]
     for copy in into:
         copy.start()
-    for n in range(3):
+    for n in range(5):
         into[n].wait()
         out[n].start()
-    for src, dst in ((gf, o_gf), (gs, o_gs)):
-        for o in range(16):
-            dst[o] = src[:, o, :].T
     for copy in out:
         copy.wait()
 
@@ -597,12 +625,17 @@
             pltpu.VMEM((3, ROWS, 256), BF),
             pltpu.VMEM((1024, 256), BF),
             pltpu.VMEM((3, 3, 128, 256), BF),
-            pltpu.VMEM((2, 192, 128), BF),
-            pltpu.VMEM((2, 192, 128), BF),
-            pltpu.VMEM((2, 160, 128), BF),
-            pltpu.VMEM((2, 160, 128), BF),
-            pltpu.VMEM((2, 2, 48, 128), BF),
-            pltpu.VMEM((2, 2, 48, 128), BF),
+            pltpu.VMEM((2, 64, 128), BF),
+            pltpu.VMEM((2, 64, 128), BF),
+            pltpu.VMEM((2, 32, 128), BF),
+            pltpu.VMEM((2, 32, 128), BF),
+            pltpu.VMEM((2, 2, 32, 128), BF),
+            pltpu.VMEM((2, 128, 128), BF),
+            pltpu.VMEM((2, 128, 128), BF),
+            pltpu.VMEM((2, 128, 128), BF),
+            pltpu.VMEM((2, 128, 128), BF),
+            pltpu.VMEM((2, 2, 16, 128), BF),
+            pltpu.VMEM((2, 2, 16, 128), BF),
             pltpu.VMEM((2, 32, 128), BF),
             pltpu.VMEM((2, 32, 128), BF),
             pltpu.VMEM((2, 16, 128), BF),
@@ -620,6 +653,13 @@
             pltpu.VMEM((32 * wide_o, 128), F32),
             pltpu.VMEM((32 * wide_o, 128), BF),
             pltpu.VMEM((zgroup, 32 * wide_o // ntz, 128), BF),
+            pltpu.VMEM((1024, 128), BF),
+            pltpu.VMEM((32, 64, 128), BF),
+            pltpu.VMEM((27, 16, 16), F32),
+            pltpu.VMEM((27, 16, 16), F32),
+            pltpu.VMEM((16, 16, 27), F32),
+            pltpu.VMEM((16, 16, 27), F32),
+            pltpu.VMEM((27, wide_o // ntz, 128), F32),
             pltpu.VMEM((3, 128, 256), F32),
             pltpu.VMEM((3, 192, 128), F32),
             pltpu.VMEM((192, 128), F32),
@@ -629,6 +669,8 @@
             pltpu.VMEM((slab, 128), F32),
             pltpu.VMEM((nty, slab, 128), F32),
             dma((7,)),
+            dma((8,)),
+            dma((8,)),
             dma((8,)),
             dma((8,)),
             dma((3,)),
@@ -645,19 +687,19 @@
             dma((zgroup,)),
             dma((nty,)),
             dma((nty,)),
+            dma((5,)),
         ]
-        vmem = pl.BlockSpec(memory_space=pltpu.VMEM)
         outs = pl.pallas_call(
             functools.partial(kernel, sizes),
             out_shape=(
                 jax.ShapeDtypeStruct((32, 64, 128), BF),
-                jax.ShapeDtypeStruct((27, 16, 16), F32),
-                jax.ShapeDtypeStruct((27, 16, 16), F32),
+                jax.ShapeDtypeStruct((16, 16, 27), F32),
+                jax.ShapeDtypeStruct((16, 16, 27), F32),
                 jax.ShapeDtypeStruct((1024, 128), BF),
                 jax.ShapeDtypeStruct((27, wide_o // ntz, 128), F32),
             ),
             in_specs=[pl.BlockSpec(memory_space=pl.ANY)] * 7,
-            out_specs=(vmem,) * 5,
+            out_specs=(pl.BlockSpec(memory_space=pl.ANY),) * 5,
             scratch_shapes=scratch,
             compiler_params=pltpu.CompilerParams(
                 collective_id=0, has_side_effects=True, vmem_limit_bytes=60 * 1024 * 1024
@@ -681,13 +723,15 @@
                 jax.ShapeDtypeStruct((1024, 128), BF),
                 jax.ShapeDtypeStruct((27, wide_o // ntz, 128), F32),
             ),
-            in_specs=[far, vmem, vmem, far, far],
-            out_specs=(far, vmem, vmem, far, far),
+            in_specs=[far] * 5,
+            out_specs=(far,) * 5,
             scratch_shapes=[
                 pltpu.VMEM((32, 64, 128), BF),
+                pltpu.VMEM((16, 16, 27), F32),
+                pltpu.VMEM((16, 16, 27), F32),
                 pltpu.VMEM((1024, 128), BF),
                 pltpu.VMEM((27, wide_o // ntz, 128), F32),
-                dma((6,)),
+                dma((10,)),
             ],
             compiler_params=pltpu.CompilerParams(vmem_limit_bytes=60 * 1024 * 1024),
         )(*outs)

time: 45.6 us -> 44.3 us (0.971); the launches traced: 45.4 us -> 43.5 us
  Pallas kernels: 44.8 us -> 42.8 us
    pallas_call x1, Pallas kernels: 3.71 us -> 2.09 us  [per_device(): pl.pallas_call(finish, out_shape=(jax.ShapeDtypeStruct((32, 64, 128), BF)...]
where the time goes in v5:
time: 44.3 us; the launch traced here: 43.5 us
  Pallas kernels  42.8 us (97%)
  between operations  0.64 us (1%)
    pallas_call x1, Pallas kernels, per_device(): pl.pallas_call(functools.partial(kernel, sizes), out_shape=(jax.ShapeDtyp...  40.7 us
    pallas_call x1, Pallas kernels, per_device(): pl.pallas_call(finish, out_shape=(jax.ShapeDtypeStruct((32, 64, 128), BF)...  2.09 us

profile of v5, /device:TPU:1, one launch (start us, length us, event | category | flops | bytes accessed | tf_op | source)
XLA Modules:
  0.0 43.5 jit_solution(8488306645816858559)
XLA Ops:
  0.6 40.7 %shard_map.110 = (bf16[32,64,128]{2,1,0:T(8,128)(2,1)}, f32[16,16,27]{2,1,0:T(8,128)}, f32[16,16,27]{2,1,0:T(8,128)}, bf16[1024,128]{1,0:T(8,128)(2,1)}, f32[27,2,128]{2,1,0:T(2,128)}) custom-call(bf16[32,64,128]{2,1,0:T(8,128)(2,1)} %bitcast.17, bf16[32,64,128]{2,1,0:T(8,128)(2,1)} %bitcast.18, bf16[256,27]{1,0:T(8,128)(2,1)} %bitcast.21, ...), custom_call_target="tpu_custom_call" | custom-call | tf_op jit(solution)/shard_map/pallas_call | solution.py:692
  41.4 2.1 %shard_map.111 = (bf16[32,64,128]{2,1,0:T(8,128)(2,1)}, f32[16,16,27]{2,1,0:T(8,128)}, f32[16,16,27]{2,1,0:T(8,128)}, bf16[1024,128]{1,0:T(8,128)(2,1)}, f32[27,2,128]{2,1,0:T(2,128)}) custom-call(bf16[32,64,128]{2,1,0:T(8,128)(2,1)} %get-tuple-element.15.refs_0_, f32[16,16,27]{2,1,0:T(8,128)} %get-tuple-element.16.refs_1_, ...), custom_call_target="tpu_custom_call" | custom-call | tf_op jit(solution)/shard_map/pallas_call | solution.py:717

commit v6 on v5

--- a/solution.py
+++ b/solution.py
@@ -320,45 +320,6 @@
             lambda t, tile=tile: zrecv[t, tile, :],
         )
 
-    version = (1, 0, 2)
-
-    def conv(n, src, g):
-        rows = pl.ds(pl.multiple_of(g * 128, 128), 192)
-        out = None
-        for cc in range(3):
-            term = mm(bands[n, cc, :, 0:192], src[version[cc], rows, :])
-            out = term if out is None else out + term
-        return out
-
-    def forward(g, carry):
-        pre = conv(0, xin, g)
-        dact = conv(1, xcot, g)
-        square = pre * pre
-        t = jnp.tanh(C0 * pre * (1.0 + C1 * square))
-        half = 0.5 + 0.5 * t
-        slope = half + 0.5 * pre * (1.0 - t * t) * (C0 * (1.0 + (3.0 * C1) * square))
-        act[pl.ds(pl.multiple_of(g * 128, 128), 128), :] = (pre * half).astype(BF)
-        xdp[0, pl.ds(pl.multiple_of(g * 128 + 32, 32), 128), :] = (dact * slope).astype(BF)
-        return carry
-
-    lax.fori_loop(0, 8, forward, 0)
-
-    columns = extract(xdp)
-    zsend2[0] = columns[0:16]
-    zsend2[1] = columns[16:32]
-    ysend2[0] = xdp[0, 32:64, 0:128]
-    ysend2[1] = xdp[0, 1024:1056, 128:256]
-    halo2 = []
-    for s in range(2):
-        halo2.append(remote(ysend2.at[s], yrecv2.at[s], gs.at[s], gr.at[s], at(step[s], 0)))
-        halo2.append(remote(zsend2.at[s], zrecv2.at[s], gs.at[2 + s], gr.at[2 + s], at(0, step[s])))
-        for t in range(2):
-            q = 4 + 2 * s + t
-            dev = at(step[s], step[t])
-            halo2.append(remote(zsend2.at[t], drecv2.at[s, t], gs.at[q], gr.at[q], dev))
-    for copy in halo2:
-        copy.start()
-
     for copy in halo_c:
         copy.wait()
     for x in range(16):
@@ -402,6 +363,41 @@
         src = rsend.at[pl.ds(9 * b, 9), :, 1 - core]
         hop0.append(remote(src, rpair.at[pl.ds(9 * b, 9)], ps.at[b], pr.at[b], other))
         hop0[b].start()
+
+    hop1 = []
+    for b in range(3):
+        hop0[b].wait()
+        for q in range(9 * b, 9 * b + 9):
+            psum[q] = (rsend[q, :, core].astype(F32) + rpair[q].astype(F32)).astype(BF)
+        for j in range(1, nx):
+            x = lax.rem(xme + j, nx)
+            src, dst = psum.at[pl.ds(9 * b, 9), x], rs1.at[xme, pl.ds(9 * b, 9)]
+            dev = (dp, 2 * x + core, tz)
+            hop1.append(remote(src, dst, r1s.at[b, j], r1r.at[b, nx - j], dev))
+            hop1[-1].start()
+
+    version = (1, 0, 2)
+
+    def conv(n, src, g):
+        rows = pl.ds(pl.multiple_of(g * 128, 128), 192)
+        out = None
+        for cc in range(3):
+            term = mm(bands[n, cc, :, 0:192], src[version[cc], rows, :])
+            out = term if out is None else out + term
+        return out
+
+    def forward(g, carry):
+        pre = conv(0, xin, g)
+        dact = conv(1, xcot, g)
+        square = pre * pre
+        t = jnp.tanh(C0 * pre * (1.0 + C1 * square))
+        half = 0.5 + 0.5 * t
+        slope = half + 0.5 * pre * (1.0 - t * t) * (C0 * (1.0 + (3.0 * C1) * square))
+        act[pl.ds(pl.multiple_of(g * 128, 128), 128), :] = (pre * half).astype(BF)
+        xdp[0, pl.ds(pl.multiple_of(g * 128 + 32, 32), 128), :] = (dact * slope).astype(BF)
+        return carry
+
+    lax.fori_loop(0, 8, forward, 0)
 
     acc1[...] = jnp.zeros_like(acc1)
     acc2[...] = jnp.zeros_like(acc2)
@@ -445,17 +441,21 @@
         copy.start()
     ar1[ty] = fpart[pl.ds(pl.multiple_of(ty * slab, 8), slab), :]
 
-    hop1 = []
-    for b in range(3):
-        hop0[b].wait()
-        for q in range(9 * b, 9 * b + 9):
-            psum[q] = (rsend[q, :, core].astype(F32) + rpair[q].astype(F32)).astype(BF)
-        for j in range(1, nx):
-            x = lax.rem(xme + j, nx)
-            src, dst = psum.at[pl.ds(9 * b, 9), x], rs1.at[xme, pl.ds(9 * b, 9)]
-            dev = (dp, 2 * x + core, tz)
-            hop1.append(remote(src, dst, r1s.at[b, j], r1r.at[b, nx - j], dev))
-            hop1[-1].start()
+    columns = extract(xdp)
+    zsend2[0] = columns[0:16]
+    zsend2[1] = columns[16:32]
+    ysend2[0] = xdp[0, 32:64, 0:128]
+    ysend2[1] = xdp[0, 1024:1056, 128:256]
+    halo2 = []
+    for s in range(2):
+        halo2.append(remote(ysend2.at[s], yrecv2.at[s], gs.at[s], gr.at[s], at(step[s], 0)))
+        halo2.append(remote(zsend2.at[s], zrecv2.at[s], gs.at[2 + s], gr.at[2 + s], at(0, step[s])))
+        for t in range(2):
+            q = 4 + 2 * s + t
+            dev = at(step[s], step[t])
+            halo2.append(remote(zsend2.at[t], drecv2.at[s, t], gs.at[q], gr.at[q], dev))
+    for copy in halo2:
+        copy.start()
 
     loads[6].wait()
 
@@ -486,6 +486,31 @@
         copy.start()
     ar2[me] = fsum1[...]
 
+    rs1[xme] = psum[:, xme]
+    for copy in hop1:
+        copy.wait()
+
+    def sum1(q, carry):
+        total = rs1[0, q].astype(F32)
+        for t in range(1, nx):
+            total = total + rs1[t, q].astype(F32)
+        k = 9 * (lax.div(q, 3) % 3) + 3 * lax.div(q, 9) + q % 3
+        qf[pl.ds(k, wide_o, stride=32), :] = total
+        return carry
+
+    lax.fori_loop(0, 27, sum1, 0)
+    qb[...] = qf[...].astype(BF)
+    deep = 32 * wide_o // ntz
+
+    hop2 = []
+    for j in range(1, zgroup):
+        g, z, dev = z_peer(j)
+        src = qb.at[pl.ds(pl.multiple_of(z * deep, 16), deep), :]
+        hop2.append(remote(src, rs2.at[me], r2s.at[j], r2r.at[zgroup - j], dev))
+    for copy in hop2:
+        copy.start()
+    rs2[me] = qb[pl.ds(pl.multiple_of(tz * deep, 16), deep), :]
+
     for copy in halo2:
         copy.wait()
     fill(
@@ -521,30 +546,15 @@
         copy.start()
     gath[ty] = fsum2[...]
 
-    rs1[xme] = psum[:, xme]
-    for copy in hop1:
-        copy.wait()
-
-    def sum1(q, carry):
-        total = rs1[0, q].astype(F32)
-        for t in range(1, nx):
-            total = total + rs1[t, q].astype(F32)
-        k = 9 * (lax.div(q, 3) % 3) + 3 * lax.div(q, 9) + q % 3
-        qf[pl.ds(k, wide_o, stride=32), :] = total
-        return carry
-
-    lax.fori_loop(0, 27, sum1, 0)
-    qb[...] = qf[...].astype(BF)
-    deep = 32 * wide_o // ntz
-
-    hop2 = []
-    for j in range(1, zgroup):
-        g, z, dev = z_peer(j)
-        src = qb.at[pl.ds(pl.multiple_of(z * deep, 16), deep), :]
-        hop2.append(remote(src, rs2.at[me], r2s.at[j], r2r.at[zgroup - j], dev))
     for copy in hop2:
-        copy.start()
-    rs2[me] = qb[pl.ds(pl.multiple_of(tz * deep, 16), deep), :]
+        copy.wait()
+    total = rs2[0].astype(F32)
+    for t in range(1, zgroup):
+        total = total + rs2[t].astype(F32)
+    for o in range(wide_o // ntz):
+        g_gc[:, o, :] = total[32 * o : 32 * o + 27, :]
+    stores.append(pltpu.make_async_copy(g_gc, o_gc, ws.at[2]))
+    stores[2].start()
 
     for copy in hop_c:
         copy.wait()
@@ -569,18 +579,8 @@
     for n, (src, mid, dst) in enumerate(((g_gf, t_gf, o_gf), (g_gs, t_gs, o_gs))):
         for o in range(16):
             mid[o] = src[:, o, :].T
-        stores.append(pltpu.make_async_copy(mid, dst, ws.at[2 + n]))
-        stores[2 + n].start()
-
-    for copy in hop2:
-        copy.wait()
-    total = rs2[0].astype(F32)
-    for t in range(1, zgroup):
-        total = total + rs2[t].astype(F32)
-    for o in range(wide_o // ntz):
-        g_gc[:, o, :] = total[32 * o : 32 * o + 27, :]
-    stores.append(pltpu.make_async_copy(g_gc, o_gc, ws.at[4]))
-    stores[4].start()
+        stores.append(pltpu.make_async_copy(mid, dst, ws.at[3 + n]))
+        stores[3 + n].start()
     for copy in stores:
         copy.wait()
 

time: 44.3 us -> 44 us (level); the launches traced: 43.5 us -> 43.8 us
  no operation moved by 1% of the time
where the time goes in v6:
time: 44 us; the launch traced here: 43.8 us
  Pallas kernels  43.2 us (98%)
  between operations  0.64 us (1%)
    pallas_call x1, Pallas kernels, per_device(): pl.pallas_call(functools.partial(kernel, sizes), out_shape=(jax.ShapeDtyp...  41.1 us
    pallas_call x1, Pallas kernels, per_device(): pl.pallas_call(finish, out_shape=(jax.ShapeDtypeStruct((32, 64, 128), BF)...  2.09 us

profile of v6, /device:TPU:1, one launch (start us, length us, event | category | flops | bytes accessed | tf_op | source)
XLA Modules:
  0.0 43.8 jit_solution(12764973625730125661)
XLA Ops:
  0.6 41.1 %shard_map.110 = (bf16[32,64,128]{2,1,0:T(8,128)(2,1)}, f32[16,16,27]{2,1,0:T(8,128)}, f32[16,16,27]{2,1,0:T(8,128)}, bf16[1024,128]{1,0:T(8,128)(2,1)}, f32[27,2,128]{2,1,0:T(2,128)}) custom-call(bf16[32,64,128]{2,1,0:T(8,128)(2,1)} %bitcast.17, bf16[32,64,128]{2,1,0:T(8,128)(2,1)} %bitcast.18, bf16[256,27]{1,0:T(8,128)(2,1)} %bitcast.21, ...), custom_call_target="tpu_custom_call" | custom-call | tf_op jit(solution)/shard_map/pallas_call | solution.py:692
  41.7 2.1 %shard_map.111 = (bf16[32,64,128]{2,1,0:T(8,128)(2,1)}, f32[16,16,27]{2,1,0:T(8,128)}, f32[16,16,27]{2,1,0:T(8,128)}, bf16[1024,128]{1,0:T(8,128)(2,1)}, f32[27,2,128]{2,1,0:T(2,128)}) custom-call(bf16[32,64,128]{2,1,0:T(8,128)(2,1)} %get-tuple-element.15.refs_0_, f32[16,16,27]{2,1,0:T(8,128)} %get-tuple-element.16.refs_1_, ...), custom_call_target="tpu_custom_call" | custom-call | tf_op jit(solution)/shard_map/pallas_call | solution.py:717

commit v7 on v6

--- a/solution.py
+++ b/solution.py
@@ -155,6 +155,11 @@
         loads.append(pltpu.make_async_copy(src, dst, ls.at[n]))
         loads[n].start()
 
+    def arrived(buf, count, ssem, rsem):
+        part = buf.at[pl.ds(0, count)]
+        for sem in (ssem, rsem):
+            pltpu.make_async_copy(part, part, sem).wait()
+
     up = (ty > 0, ty < nty - 1)
     side = (tz > 0, tz < ntz - 1)
 
@@ -373,7 +378,7 @@
             x = lax.rem(xme + j, nx)
             src, dst = psum.at[pl.ds(9 * b, 9), x], rs1.at[xme, pl.ds(9 * b, 9)]
             dev = (dp, 2 * x + core, tz)
-            hop1.append(remote(src, dst, r1s.at[b, j], r1r.at[b, nx - j], dev))
+            hop1.append(remote(src, dst, r1s.at[0], r1r.at[0], dev))
             hop1[-1].start()
 
     version = (1, 0, 2)
@@ -386,7 +391,7 @@
             out = term if out is None else out + term
         return out
 
-    def forward(g, carry):
+    def forward(g):
         pre = conv(0, xin, g)
         dact = conv(1, xcot, g)
         square = pre * pre
@@ -395,23 +400,24 @@
         slope = half + 0.5 * pre * (1.0 - t * t) * (C0 * (1.0 + (3.0 * C1) * square))
         act[pl.ds(pl.multiple_of(g * 128, 128), 128), :] = (pre * half).astype(BF)
         xdp[0, pl.ds(pl.multiple_of(g * 128 + 32, 32), 128), :] = (dact * slope).astype(BF)
+
+    def four(i, carry):
+        for q in range(4):
+            forward(4 * i + q)
         return carry
 
-    lax.fori_loop(0, 8, forward, 0)
-
-    acc1[...] = jnp.zeros_like(acc1)
-    acc2[...] = jnp.zeros_like(acc2)
-
-    def gram(g, carry):
-        rows = pl.ds(pl.multiple_of(g * 128, 128), 192)
-        own = xdp[0, pl.ds(pl.multiple_of(g * 128 + 32, 32), 128), :]
-        a_own = act[pl.ds(pl.multiple_of(g * 128, 128), 128), :]
-        for cc in range(3):
-            acc1[cc, :, 0:192] += mm(own, xin[version[cc], rows, :], NT)
-            acc2[cc] += mm(xcot[version[cc], rows, :], a_own, NT)
-        return carry
-
-    lax.fori_loop(0, 8, gram, 0)
+    lax.fori_loop(0, 2, four, 0)
+
+    def groups(ref, lead, first, count):
+        return jnp.concatenate(
+            [ref[(*lead, slice(128 * g + first, 128 * g + first + count))] for g in range(8)], 1
+        )
+
+    own, a_own = groups(xdp, (0,), 32, 128), groups(act, (), 0, 128)
+    for cc in range(3):
+        acc1[cc, :, 0:192] = mm(own, groups(xin, (version[cc],), 0, 192), NT)
+        acc1[cc, :, 192:256] = jnp.zeros((128, 64), F32)
+        acc2[cc] = mm(groups(xcot, (version[cc],), 0, 192), a_own, NT)
     for cc in range(3):
         total = None
         for yo in range(4):
@@ -436,7 +442,7 @@
     for j in range(1, nty):
         t, dev = ty_peer(j)
         src = fpart.at[pl.ds(pl.multiple_of(t * slab, 8), slab), :]
-        hop_a.append(remote(src, ar1.at[ty], a1s.at[j], a1r.at[nty - j], dev))
+        hop_a.append(remote(src, ar1.at[ty], a1s.at[0], a1r.at[0], dev))
     for copy in hop_a:
         copy.start()
     ar1[ty] = fpart[pl.ds(pl.multiple_of(ty * slab, 8), slab), :]
@@ -459,21 +465,16 @@
 
     loads[6].wait()
 
-    def coarse(q, carry):
-        out = None
-        for a in range(3):
-            left = vmat[pl.ds(q * 4 + 2 - a, 4)].reshape(256, 1152)
-            term = mm(left, wc[1152 * a : 1152 * a + 1152, :])
-            out = term if out is None else out + term
-        g_gci[pl.ds(pl.multiple_of(q * 256, 256), 256), :] = out.astype(BF)
-        return carry
-
-    lax.fori_loop(0, 4, coarse, 0)
+    out = None
+    for a in range(3):
+        left = vmat[2 - a : 18 - a].reshape(1024, 1152)
+        term = mm(left, wc[1152 * a : 1152 * a + 1152, :])
+        out = term if out is None else out + term
+    g_gci[...] = out.astype(BF)
     stores = [pltpu.make_async_copy(g_gci, o_gci, ws.at[0])]
     stores[0].start()
 
-    for copy in hop_a:
-        copy.wait()
+    arrived(ar1, nty - 1, a1s.at[0], a1r.at[0])
     total = ar1[0]
     for t in range(1, nty):
         total = total + ar1[t]
@@ -481,14 +482,13 @@
     hop_b = []
     for j in range(1, zgroup):
         g, z, dev = z_peer(j)
-        hop_b.append(remote(fsum1, ar2.at[me], a2s.at[j], a2r.at[zgroup - j], dev))
+        hop_b.append(remote(fsum1, ar2.at[me], a2s.at[0], a2r.at[0], dev))
     for copy in hop_b:
         copy.start()
     ar2[me] = fsum1[...]
 
     rs1[xme] = psum[:, xme]
-    for copy in hop1:
-        copy.wait()
+    arrived(rs1, nx - 1, r1s.at[0], r1r.at[0])
 
     def sum1(q, carry):
         total = rs1[0, q].astype(F32)
@@ -506,7 +506,7 @@
     for j in range(1, zgroup):
         g, z, dev = z_peer(j)
         src = qb.at[pl.ds(pl.multiple_of(z * deep, 16), deep), :]
-        hop2.append(remote(src, rs2.at[me], r2s.at[j], r2r.at[zgroup - j], dev))
+        hop2.append(remote(src, rs2.at[me], r2s.at[0], r2r.at[0], dev))
     for copy in hop2:
         copy.start()
     rs2[me] = qb[pl.ds(pl.multiple_of(tz * deep, 16), deep), :]
@@ -532,8 +532,7 @@
     stores.append(pltpu.make_async_copy(g_gfi, o_gfi, ws.at[1]))
     stores[1].start()
 
-    for copy in hop_b:
-        copy.wait()
+    arrived(ar2, zgroup - 1, a2s.at[0], a2r.at[0])
     total = ar2[0]
     for t in range(1, zgroup):
         total = total + ar2[t]
@@ -541,13 +540,12 @@
     hop_c = []
     for j in range(1, nty):
         t, dev = ty_peer(j)
-        hop_c.append(remote(fsum2, gath.at[ty], a3s.at[j], a3r.at[nty - j], dev))
+        hop_c.append(remote(fsum2, gath.at[ty], a3s.at[0], a3r.at[0], dev))
     for copy in hop_c:
         copy.start()
     gath[ty] = fsum2[...]
 
-    for copy in hop2:
-        copy.wait()
+    arrived(rs2, zgroup - 1, r2s.at[0], r2r.at[0])
     total = rs2[0].astype(F32)
     for t in range(1, zgroup):
         total = total + rs2[t].astype(F32)
@@ -556,8 +554,7 @@
     stores.append(pltpu.make_async_copy(g_gc, o_gc, ws.at[2]))
     stores[2].start()
 
-    for copy in hop_c:
-        copy.wait()
+    arrived(gath, nty - 1, a3s.at[0], a3r.at[0])
     fpart[...] = gath[...].reshape(192, 128)
     for a in range(3):
         planes = [(xo, xo + a - 1) for xo in range(2) if 0 <= xo + a - 1 < 2]
@@ -677,16 +674,16 @@
             dma((3,)),
             dma((8,)),
             dma((8,)),
-            dma((3, nx)),
-            dma((3, nx)),
-            dma((zgroup,)),
-            dma((zgroup,)),
-            dma((nty,)),
-            dma((nty,)),
-            dma((zgroup,)),
-            dma((zgroup,)),
-            dma((nty,)),
-            dma((nty,)),
+            dma((1,)),
+            dma((1,)),
+            dma((1,)),
+            dma((1,)),
+            dma((1,)),
+            dma((1,)),
+            dma((1,)),
+            dma((1,)),
+            dma((1,)),
+            dma((1,)),
             dma((5,)),
         ]
         outs = pl.pallas_call(

time: 44 us -> 41.1 us (0.934)
  Pallas kernels: 43.2 us -> 40.4 us
    pallas_call x1, Pallas kernels: 41.1 us -> 38.3 us  [per_device(): pl.pallas_call(functools.partial(kernel, sizes), out_shape=(jax.ShapeDtyp...]
where the time goes in v7:
time: 41.1 us; the launch traced here: 41 us
  Pallas kernels  40.4 us (98%)
  between operations  0.64 us (2%)
    pallas_call x1, Pallas kernels, per_device(): pl.pallas_call(functools.partial(kernel, sizes), out_shape=(jax.ShapeDtyp...  38.3 us
    pallas_call x1, Pallas kernels, per_device(): pl.pallas_call(finish, out_shape=(jax.ShapeDtypeStruct((32, 64, 128), BF)...  2.09 us

profile of v7, /device:TPU:1, one launch (start us, length us, event | category | flops | bytes accessed | tf_op | source)
XLA Modules:
  0.0 41.0 jit_solution(1865651783828569769)
XLA Ops:
  0.6 38.3 %shard_map.110 = (bf16[32,64,128]{2,1,0:T(8,128)(2,1)}, f32[16,16,27]{2,1,0:T(8,128)}, f32[16,16,27]{2,1,0:T(8,128)}, bf16[1024,128]{1,0:T(8,128)(2,1)}, f32[27,2,128]{2,1,0:T(2,128)}) custom-call(bf16[32,64,128]{2,1,0:T(8,128)(2,1)} %bitcast.17, bf16[32,64,128]{2,1,0:T(8,128)(2,1)} %bitcast.18, bf16[256,27]{1,0:T(8,128)(2,1)} %bitcast.21, ...), custom_call_target="tpu_custom_call" | custom-call | tf_op jit(solution)/shard_map/pallas_call | solution.py:689
  38.9 2.1 %shard_map.111 = (bf16[32,64,128]{2,1,0:T(8,128)(2,1)}, f32[16,16,27]{2,1,0:T(8,128)}, f32[16,16,27]{2,1,0:T(8,128)}, bf16[1024,128]{1,0:T(8,128)(2,1)}, f32[27,2,128]{2,1,0:T(2,128)}) custom-call(bf16[32,64,128]{2,1,0:T(8,128)(2,1)} %get-tuple-element.15.refs_0_, f32[16,16,27]{2,1,0:T(8,128)} %get-tuple-element.16.refs_1_, ...), custom_call_target="tpu_custom_call" | custom-call | tf_op jit(solution)/shard_map/pallas_call | solution.py:714

commit v8 on v7

--- a/solution.py
+++ b/solution.py
@@ -149,12 +149,6 @@
             device_id_type=MESH,
         )
 
-    loads = []
-    pairs = ((h_ccot, ccot), (h_fin, fin), (h_fcot, fcot), (h_w1, w1), (h_w2, w2), (h_cin, cin), (h_wc, wc))
-    for n, (src, dst) in enumerate(pairs):
-        loads.append(pltpu.make_async_copy(src, dst, ls.at[n]))
-        loads[n].start()
-
     def arrived(buf, count, ssem, rsem):
         part = buf.at[pl.ds(0, count)]
         for sem in (ssem, rsem):
@@ -169,6 +163,12 @@
     partners += [z_peer(j)[2] for j in range(1, zgroup)]
     for dev in partners:
         pl.semaphore_signal(barrier, inc=1, device_id=dev, device_id_type=MESH)
+
+    loads = []
+    pairs = ((h_ccot, ccot), (h_fin, fin), (h_fcot, fcot), (h_w1, w1), (h_w2, w2), (h_cin, cin), (h_wc, wc))
+    for n, (src, dst) in enumerate(pairs):
+        loads.append(pltpu.make_async_copy(src, dst, ls.at[n]))
+        loads[n].start()
 
     r, c = iota((512, 512), 0), iota((512, 512), 1)
     perm[...] = one_hot(c == (r % 16) * 32 + ((r // 16) % 2) * 16 + r // 32)
@@ -316,14 +316,16 @@
             dst[v, 0:32, 128:256] = dst[v, 1024:1056, 0:128]
             dst[v, 1056:1088, 0:128] = dst[v, 32:64, 128:256]
 
-    for n, dst in enumerate((xin, xcot)):
+    def fill_first(n, dst):
         rows, tile = slice(32 * n, 32 * n + 32), slice(16 * n, 16 * n + 16)
         fill(
             dst,
-            lambda s, rows=rows: yrecv[s, rows, :],
-            lambda s, t, tile=tile: drecv[s, t, tile, :],
-            lambda t, tile=tile: zrecv[t, tile, :],
+            lambda s: yrecv[s, rows, :],
+            lambda s, t: drecv[s, t, tile, :],
+            lambda t: zrecv[t, tile, :],
         )
+
+    fill_first(0, xin)
 
     for copy in halo_c:
         copy.wait()
@@ -358,16 +360,18 @@
     core, xme = lax.rem(ty, 2), lax.div(ty, 2)
     other = (dp, ty + 1 - 2 * core, tz)
     hop0 = []
+    g = mm(vmat[...].reshape(1152, 1152), inp3[...], TN)
     for b in range(3):
-        left = vmat[:, :, 384 * b : 384 * b + 384].reshape(1152, 384)
-        g = mm(left, inp3[...], TN)
         for a in range(3):
             for cc in range(3):
-                part = g[128 * cc : 128 * cc + 128, 128 * a : 128 * a + 128]
+                first = 384 * b + 128 * cc
+                part = g[first : first + 128, 128 * a : 128 * a + 128]
                 rsend[9 * b + 3 * a + cc] = part.astype(BF).reshape(nx, 2, wide_o, 128)
         src = rsend.at[pl.ds(9 * b, 9), :, 1 - core]
         hop0.append(remote(src, rpair.at[pl.ds(9 * b, 9)], ps.at[b], pr.at[b], other))
         hop0[b].start()
+
+    fill_first(1, xcot)
 
     hop1 = []
     for b in range(3):
@@ -584,13 +588,16 @@
 
 def finish(*refs):
     srcs, dsts, mids, sems = refs[:5], refs[5:10], refs[10:15], refs[15]
-    into = [pltpu.make_async_copy(srcs[n], mids[n], sems.at[n]) for n in range(5)]
-    out = [pltpu.make_async_copy(mids[n], dsts[n], sems.at[5 + n]) for n in range(5)]
-    for copy in into:
-        copy.start()
-    for n in range(5):
-        into[n].wait()
-        out[n].start()
+    pieces = [(0, pl.ds(8 * q, 8)) for q in range(4)] + [(3, pl.ds(512 * q, 512)) for q in range(2)]
+    pieces += [(n, pl.ds(0, srcs[n].shape[0])) for n in (1, 2, 4)]
+    into, out = [], []
+    for q, (n, rows) in enumerate(pieces):
+        into.append(pltpu.make_async_copy(srcs[n].at[rows], mids[n].at[rows], sems.at[0, q]))
+        out.append(pltpu.make_async_copy(mids[n].at[rows], dsts[n].at[rows], sems.at[1, q]))
+        into[q].start()
+    for q in range(len(pieces)):
+        into[q].wait()
+        out[q].start()
     for copy in out:
         copy.wait()
 
@@ -728,7 +735,7 @@
                 pltpu.VMEM((16, 16, 27), F32),
                 pltpu.VMEM((1024, 128), BF),
                 pltpu.VMEM((27, wide_o // ntz, 128), F32),
-                dma((10,)),
+                dma((2, 9)),
             ],
             compiler_params=pltpu.CompilerParams(vmem_limit_bytes=60 * 1024 * 1024),
         )(*outs)

time: 41.1 us -> 41.5 us (level)
  no operation moved by 1% of the time
where the time goes in v8:
time: 41.5 us; the launch traced here: 41.3 us
  Pallas kernels  40.7 us (98%)
  between operations  0.64 us (2%)
    pallas_call x1, Pallas kernels, per_device(): pl.pallas_call(functools.partial(kernel, sizes), out_shape=(jax.ShapeDtyp...  38.6 us
    pallas_call x1, Pallas kernels, per_device(): pl.pallas_call(finish, out_shape=(jax.ShapeDtypeStruct((32, 64, 128), BF)...  2.11 us

profile of v8, /device:TPU:1, one launch (start us, length us, event | category | flops | bytes accessed | tf_op | source)
XLA Modules:
  0.0 41.3 jit_solution(5112327288992890178)
XLA Ops:
  0.6 38.6 %shard_map.110 = (bf16[32,64,128]{2,1,0:T(8,128)(2,1)}, f32[16,16,27]{2,1,0:T(8,128)}, f32[16,16,27]{2,1,0:T(8,128)}, bf16[1024,128]{1,0:T(8,128)(2,1)}, f32[27,2,128]{2,1,0:T(2,128)}) custom-call(bf16[32,64,128]{2,1,0:T(8,128)(2,1)} %bitcast.17, bf16[32,64,128]{2,1,0:T(8,128)(2,1)} %bitcast.18, bf16[256,27]{1,0:T(8,128)(2,1)} %bitcast.21, ...), custom_call_target="tpu_custom_call" | custom-call | tf_op jit(solution)/shard_map/pallas_call | solution.py:696
  39.2 2.1 %shard_map.111 = (bf16[32,64,128]{2,1,0:T(8,128)(2,1)}, f32[16,16,27]{2,1,0:T(8,128)}, f32[16,16,27]{2,1,0:T(8,128)}, bf16[1024,128]{1,0:T(8,128)(2,1)}, f32[27,2,128]{2,1,0:T(2,128)}) custom-call(bf16[32,64,128]{2,1,0:T(8,128)(2,1)} %get-tuple-element.15.refs_0_, f32[16,16,27]{2,1,0:T(8,128)} %get-tuple-element.16.refs_1_, ...), custom_call_target="tpu_custom_call" | custom-call | tf_op jit(solution)/shard_map/pallas_call | solution.py:721

commit v9 on v8

--- a/solution.py
+++ b/solution.py
@@ -373,8 +373,29 @@
 
     fill_first(1, xcot)
 
+    version = (1, 0, 2)
+
+    def conv(n, src, g):
+        rows = pl.ds(pl.multiple_of(g * 128, 128), 192)
+        out = None
+        for cc in range(3):
+            term = mm(bands[n, cc, :, 0:192], src[version[cc], rows, :])
+            out = term if out is None else out + term
+        return out
+
+    def forward(g):
+        pre = conv(0, xin, g)
+        dact = conv(1, xcot, g)
+        square = pre * pre
+        t = jnp.tanh(C0 * pre * (1.0 + C1 * square))
+        half = 0.5 + 0.5 * t
+        slope = half + 0.5 * pre * (1.0 - t * t) * (C0 * (1.0 + (3.0 * C1) * square))
+        act[pl.ds(pl.multiple_of(g * 128, 128), 128), :] = (pre * half).astype(BF)
+        xdp[0, pl.ds(pl.multiple_of(g * 128 + 32, 32), 128), :] = (dact * slope).astype(BF)
+
     hop1 = []
-    for b in range(3):
+
+    def send_sum(b):
         hop0[b].wait()
         for q in range(9 * b, 9 * b + 9):
             psum[q] = (rsend[q, :, core].astype(F32) + rpair[q].astype(F32)).astype(BF)
@@ -385,32 +406,12 @@
             hop1.append(remote(src, dst, r1s.at[0], r1r.at[0], dev))
             hop1[-1].start()
 
-    version = (1, 0, 2)
-
-    def conv(n, src, g):
-        rows = pl.ds(pl.multiple_of(g * 128, 128), 192)
-        out = None
-        for cc in range(3):
-            term = mm(bands[n, cc, :, 0:192], src[version[cc], rows, :])
-            out = term if out is None else out + term
-        return out
-
-    def forward(g):
-        pre = conv(0, xin, g)
-        dact = conv(1, xcot, g)
-        square = pre * pre
-        t = jnp.tanh(C0 * pre * (1.0 + C1 * square))
-        half = 0.5 + 0.5 * t
-        slope = half + 0.5 * pre * (1.0 - t * t) * (C0 * (1.0 + (3.0 * C1) * square))
-        act[pl.ds(pl.multiple_of(g * 128, 128), 128), :] = (pre * half).astype(BF)
-        xdp[0, pl.ds(pl.multiple_of(g * 128 + 32, 32), 128), :] = (dact * slope).astype(BF)
-
-    def four(i, carry):
-        for q in range(4):
-            forward(4 * i + q)
-        return carry
-
-    lax.fori_loop(0, 2, four, 0)
+    send_sum(0)
+    for g in range(8):
+        forward(g)
+        if g == 3:
+            send_sum(1)
+    send_sum(2)
 
     def groups(ref, lead, first, count):
         return jnp.concatenate(
@@ -491,6 +492,15 @@
         copy.start()
     ar2[me] = fsum1[...]
 
+    for copy in halo2:
+        copy.wait()
+    fill(
+        xdp,
+        lambda s: yrecv2[s],
+        lambda s, t: drecv2[s, t],
+        lambda t: zrecv2[t],
+    )
+
     rs1[xme] = psum[:, xme]
     arrived(rs1, nx - 1, r1s.at[0], r1r.at[0])
 
@@ -514,15 +524,6 @@
     for copy in hop2:
         copy.start()
     rs2[me] = qb[pl.ds(pl.multiple_of(tz * deep, 16), deep), :]
-
-    for copy in halo2:
-        copy.wait()
-    fill(
-        xdp,
-        lambda s: yrecv2[s],
-        lambda s, t: drecv2[s, t],
-        lambda t: zrecv2[t],
-    )
 
     def last(j, carry):
         parts = [conv(2, xdp, 4 * j + q).astype(BF) for q in range(4)]

time: 41.5 us -> 40.9 us (0.986)
  Pallas kernels: 40.7 us -> 40.1 us
    pallas_call x1, Pallas kernels: 38.6 us -> 38 us  [per_device(): pl.pallas_call(functools.partial(kernel, sizes), out_shape=(jax.ShapeDtyp...]
where the time goes in v9:
time: 40.9 us; the launch traced here: 40.7 us
  Pallas kernels  40.1 us (98%)
  between operations  0.64 us (2%)
    pallas_call x1, Pallas kernels, per_device(): pl.pallas_call(functools.partial(kernel, sizes), out_shape=(jax.ShapeDtyp...  38 us
    pallas_call x1, Pallas kernels, per_device(): pl.pallas_call(finish, out_shape=(jax.ShapeDtypeStruct((32, 64, 128), BF)...  2.11 us

profile of v9, /device:TPU:1, one launch (start us, length us, event | category | flops | bytes accessed | tf_op | source)
XLA Modules:
  0.0 40.7 jit_solution(5182226882528510356)
XLA Ops:
  0.6 38.0 %shard_map.110 = (bf16[32,64,128]{2,1,0:T(8,128)(2,1)}, f32[16,16,27]{2,1,0:T(8,128)}, f32[16,16,27]{2,1,0:T(8,128)}, bf16[1024,128]{1,0:T(8,128)(2,1)}, f32[27,2,128]{2,1,0:T(2,128)}) custom-call(bf16[32,64,128]{2,1,0:T(8,128)(2,1)} %bitcast.17, bf16[32,64,128]{2,1,0:T(8,128)(2,1)} %bitcast.18, bf16[256,27]{1,0:T(8,128)(2,1)} %bitcast.21, ...), custom_call_target="tpu_custom_call" | custom-call | tf_op jit(solution)/shard_map/pallas_call | solution.py:697
  38.6 2.1 %shard_map.111 = (bf16[32,64,128]{2,1,0:T(8,128)(2,1)}, f32[16,16,27]{2,1,0:T(8,128)}, f32[16,16,27]{2,1,0:T(8,128)}, bf16[1024,128]{1,0:T(8,128)(2,1)}, f32[27,2,128]{2,1,0:T(2,128)}) custom-call(bf16[32,64,128]{2,1,0:T(8,128)(2,1)} %get-tuple-element.15.refs_0_, f32[16,16,27]{2,1,0:T(8,128)} %get-tuple-element.16.refs_1_, ...), custom_call_target="tpu_custom_call" | custom-call | tf_op jit(solution)/shard_map/pallas_call | solution.py:722

commit v10 on v9

--- a/solution.py
+++ b/solution.py
@@ -326,51 +326,6 @@
         )
 
     fill_first(0, xin)
-
-    for copy in halo_c:
-        copy.wait()
-    for x in range(16):
-        rows = slice(8 * (x // 2 * 2), 16 + 8 * (x // 2 * 2))
-        half = slice(8 * (x % 2), 8 * (x % 2) + 8)
-        cflat[80 * x : 80 * x + 8, :] = valid(up[0], ycr[1, rows, :].astype(F32)[half])
-        cflat[80 * x + 72 : 80 * x + 80, :] = valid(up[1], ycr[0, rows, :].astype(F32)[half])
-    cplus[...] = pltpu.roll(cflat[...], 1279, 0)
-    cminus[...] = pltpu.roll(cflat[...], 1, 0)
-    for y in range(10):
-        for ref, z, t, ok in ((cplus, 7, 0, side[1]), (cminus, 0, 1, side[0])):
-            if y == 0:
-                part, ok = dcr[1, t], ok & up[0]
-            elif y == 9:
-                part, ok = dcr[0, t], ok & up[1]
-            else:
-                part = zcr[t, 16 * (y - 1) : 16 * y, :]
-            ref[pl.ds(8 * y + z, 16, stride=80), :] = valid(ok, part.astype(F32))
-
-    def spread(x, carry):
-        for b in range(3):
-            for cc, ref in enumerate((cplus, cflat, cminus)):
-                rows = ref[pl.ds(pl.multiple_of(x * 80 + 8 * (2 - b), 8), 64), :]
-                q = 3 * b + cc
-                vmat[x + 1, :, 128 * q : 128 * q + 128] = rows.astype(BF)
-        return carry
-
-    lax.fori_loop(0, 16, spread, 0)
-
-    wide_o, nx = 128 // nty, nty // 2
-    core, xme = lax.rem(ty, 2), lax.div(ty, 2)
-    other = (dp, ty + 1 - 2 * core, tz)
-    hop0 = []
-    g = mm(vmat[...].reshape(1152, 1152), inp3[...], TN)
-    for b in range(3):
-        for a in range(3):
-            for cc in range(3):
-                first = 384 * b + 128 * cc
-                part = g[first : first + 128, 128 * a : 128 * a + 128]
-                rsend[9 * b + 3 * a + cc] = part.astype(BF).reshape(nx, 2, wide_o, 128)
-        src = rsend.at[pl.ds(9 * b, 9), :, 1 - core]
-        hop0.append(remote(src, rpair.at[pl.ds(9 * b, 9)], ps.at[b], pr.at[b], other))
-        hop0[b].start()
-
     fill_first(1, xcot)
 
     version = (1, 0, 2)
@@ -393,25 +348,8 @@
         act[pl.ds(pl.multiple_of(g * 128, 128), 128), :] = (pre * half).astype(BF)
         xdp[0, pl.ds(pl.multiple_of(g * 128 + 32, 32), 128), :] = (dact * slope).astype(BF)
 
-    hop1 = []
-
-    def send_sum(b):
-        hop0[b].wait()
-        for q in range(9 * b, 9 * b + 9):
-            psum[q] = (rsend[q, :, core].astype(F32) + rpair[q].astype(F32)).astype(BF)
-        for j in range(1, nx):
-            x = lax.rem(xme + j, nx)
-            src, dst = psum.at[pl.ds(9 * b, 9), x], rs1.at[xme, pl.ds(9 * b, 9)]
-            dev = (dp, 2 * x + core, tz)
-            hop1.append(remote(src, dst, r1s.at[0], r1r.at[0], dev))
-            hop1[-1].start()
-
-    send_sum(0)
     for g in range(8):
         forward(g)
-        if g == 3:
-            send_sum(1)
-    send_sum(2)
 
     def groups(ref, lead, first, count):
         return jnp.concatenate(
@@ -468,16 +406,49 @@
     for copy in halo2:
         copy.start()
 
-    loads[6].wait()
-
-    out = None
-    for a in range(3):
-        left = vmat[2 - a : 18 - a].reshape(1024, 1152)
-        term = mm(left, wc[1152 * a : 1152 * a + 1152, :])
-        out = term if out is None else out + term
-    g_gci[...] = out.astype(BF)
-    stores = [pltpu.make_async_copy(g_gci, o_gci, ws.at[0])]
-    stores[0].start()
+    for copy in halo_c:
+        copy.wait()
+    for x in range(16):
+        rows = slice(8 * (x // 2 * 2), 16 + 8 * (x // 2 * 2))
+        half = slice(8 * (x % 2), 8 * (x % 2) + 8)
+        cflat[80 * x : 80 * x + 8, :] = valid(up[0], ycr[1, rows, :].astype(F32)[half])
+        cflat[80 * x + 72 : 80 * x + 80, :] = valid(up[1], ycr[0, rows, :].astype(F32)[half])
+    cplus[...] = pltpu.roll(cflat[...], 1279, 0)
+    cminus[...] = pltpu.roll(cflat[...], 1, 0)
+    for y in range(10):
+        for ref, z, t, ok in ((cplus, 7, 0, side[1]), (cminus, 0, 1, side[0])):
+            if y == 0:
+                part, ok = dcr[1, t], ok & up[0]
+            elif y == 9:
+                part, ok = dcr[0, t], ok & up[1]
+            else:
+                part = zcr[t, 16 * (y - 1) : 16 * y, :]
+            ref[pl.ds(8 * y + z, 16, stride=80), :] = valid(ok, part.astype(F32))
+
+    def spread(x, carry):
+        for b in range(3):
+            for cc, ref in enumerate((cplus, cflat, cminus)):
+                rows = ref[pl.ds(pl.multiple_of(x * 80 + 8 * (2 - b), 8), 64), :]
+                q = 3 * b + cc
+                vmat[x + 1, :, 128 * q : 128 * q + 128] = rows.astype(BF)
+        return carry
+
+    lax.fori_loop(0, 16, spread, 0)
+
+    wide_o, nx = 128 // nty, nty // 2
+    core, xme = lax.rem(ty, 2), lax.div(ty, 2)
+    other = (dp, ty + 1 - 2 * core, tz)
+    hop0 = []
+    g = mm(vmat[...].reshape(1152, 1152), inp3[...], TN)
+    for b in range(3):
+        for a in range(3):
+            for cc in range(3):
+                first = 384 * b + 128 * cc
+                part = g[first : first + 128, 128 * a : 128 * a + 128]
+                rsend[9 * b + 3 * a + cc] = part.astype(BF).reshape(nx, 2, wide_o, 128)
+        src = rsend.at[pl.ds(9 * b, 9), :, 1 - core]
+        hop0.append(remote(src, rpair.at[pl.ds(9 * b, 9)], ps.at[b], pr.at[b], other))
+        hop0[b].start()
 
     arrived(ar1, nty - 1, a1s.at[0], a1r.at[0])
     total = ar1[0]
@@ -492,6 +463,33 @@
         copy.start()
     ar2[me] = fsum1[...]
 
+    hop1 = []
+
+    def send_sum(b):
+        hop0[b].wait()
+        for q in range(9 * b, 9 * b + 9):
+            psum[q] = (rsend[q, :, core].astype(F32) + rpair[q].astype(F32)).astype(BF)
+        for j in range(1, nx):
+            x = lax.rem(xme + j, nx)
+            src, dst = psum.at[pl.ds(9 * b, 9), x], rs1.at[xme, pl.ds(9 * b, 9)]
+            dev = (dp, 2 * x + core, tz)
+            hop1.append(remote(src, dst, r1s.at[0], r1r.at[0], dev))
+            hop1[-1].start()
+
+    for b in range(3):
+        send_sum(b)
+
+    loads[6].wait()
+
+    out = None
+    for a in range(3):
+        left = vmat[2 - a : 18 - a].reshape(1024, 1152)
+        term = mm(left, wc[1152 * a : 1152 * a + 1152, :])
+        out = term if out is None else out + term
+    g_gci[...] = out.astype(BF)
+    stores = [pltpu.make_async_copy(g_gci, o_gci, ws.at[0])]
+    stores[0].start()
+
     for copy in halo2:
         copy.wait()
     fill(
@@ -500,42 +498,6 @@
         lambda s, t: drecv2[s, t],
         lambda t: zrecv2[t],
     )
-
-    rs1[xme] = psum[:, xme]
-    arrived(rs1, nx - 1, r1s.at[0], r1r.at[0])
-
-    def sum1(q, carry):
-        total = rs1[0, q].astype(F32)
-        for t in range(1, nx):
-            total = total + rs1[t, q].astype(F32)
-        k = 9 * (lax.div(q, 3) % 3) + 3 * lax.div(q, 9) + q % 3
-        qf[pl.ds(k, wide_o, stride=32), :] = total
-        return carry
-
-    lax.fori_loop(0, 27, sum1, 0)
-    qb[...] = qf[...].astype(BF)
-    deep = 32 * wide_o // ntz
-
-    hop2 = []
-    for j in range(1, zgroup):
-        g, z, dev = z_peer(j)
-        src = qb.at[pl.ds(pl.multiple_of(z * deep, 16), deep), :]
-        hop2.append(remote(src, rs2.at[me], r2s.at[0], r2r.at[0], dev))
-    for copy in hop2:
-        copy.start()
-    rs2[me] = qb[pl.ds(pl.multiple_of(tz * deep, 16), deep), :]
-
-    def last(j, carry):
-        parts = [conv(2, xdp, 4 * j + q).astype(BF) for q in range(4)]
-        out = mm(perm[...], jnp.concatenate(parts, 0)).astype(BF)
-        first = pl.multiple_of(16 * j, 16)
-        g_gfi[:, pl.ds(first, 16), :] = out[:, :128].reshape(32, 16, 128)
-        g_gfi[:, pl.ds(first + 32, 16), :] = out[:, 128:].reshape(32, 16, 128)
-        return carry
-
-    lax.fori_loop(0, 2, last, 0)
-    stores.append(pltpu.make_async_copy(g_gfi, o_gfi, ws.at[1]))
-    stores[1].start()
 
     arrived(ar2, zgroup - 1, a2s.at[0], a2r.at[0])
     total = ar2[0]
@@ -550,14 +512,41 @@
         copy.start()
     gath[ty] = fsum2[...]
 
-    arrived(rs2, zgroup - 1, r2s.at[0], r2r.at[0])
-    total = rs2[0].astype(F32)
-    for t in range(1, zgroup):
-        total = total + rs2[t].astype(F32)
-    for o in range(wide_o // ntz):
-        g_gc[:, o, :] = total[32 * o : 32 * o + 27, :]
-    stores.append(pltpu.make_async_copy(g_gc, o_gc, ws.at[2]))
-    stores[2].start()
+    def last(j, carry):
+        parts = [conv(2, xdp, 4 * j + q).astype(BF) for q in range(4)]
+        out = mm(perm[...], jnp.concatenate(parts, 0)).astype(BF)
+        first = pl.multiple_of(16 * j, 16)
+        g_gfi[:, pl.ds(first, 16), :] = out[:, :128].reshape(32, 16, 128)
+        g_gfi[:, pl.ds(first + 32, 16), :] = out[:, 128:].reshape(32, 16, 128)
+        return carry
+
+    lax.fori_loop(0, 2, last, 0)
+    stores.append(pltpu.make_async_copy(g_gfi, o_gfi, ws.at[1]))
+    stores[1].start()
+
+    rs1[xme] = psum[:, xme]
+    arrived(rs1, nx - 1, r1s.at[0], r1r.at[0])
+
+    def sum1(q, carry):
+        total = rs1[0, q].astype(F32)
+        for t in range(1, nx):
+            total = total + rs1[t, q].astype(F32)
+        k = 9 * (lax.div(q, 3) % 3) + 3 * lax.div(q, 9) + q % 3
+        qf[pl.ds(k, wide_o, stride=32), :] = total
+        return carry
+
+    lax.fori_loop(0, 27, sum1, 0)
+    qb[...] = qf[...].astype(BF)
+    deep = 32 * wide_o // ntz
+
+    hop2 = []
+    for j in range(1, zgroup):
+        g, z, dev = z_peer(j)
+        src = qb.at[pl.ds(pl.multiple_of(z * deep, 16), deep), :]
+        hop2.append(remote(src, rs2.at[me], r2s.at[0], r2r.at[0], dev))
+    for copy in hop2:
+        copy.start()
+    rs2[me] = qb[pl.ds(pl.multiple_of(tz * deep, 16), deep), :]
 
     arrived(gath, nty - 1, a3s.at[0], a3r.at[0])
     fpart[...] = gath[...].reshape(192, 128)
@@ -581,8 +570,17 @@
     for n, (src, mid, dst) in enumerate(((g_gf, t_gf, o_gf), (g_gs, t_gs, o_gs))):
         for o in range(16):
             mid[o] = src[:, o, :].T
-        stores.append(pltpu.make_async_copy(mid, dst, ws.at[3 + n]))
-        stores[3 + n].start()
+        stores.append(pltpu.make_async_copy(mid, dst, ws.at[2 + n]))
+        stores[2 + n].start()
+
+    arrived(rs2, zgroup - 1, r2s.at[0], r2r.at[0])
+    total = rs2[0].astype(F32)
+    for t in range(1, zgroup):
+        total = total + rs2[t].astype(F32)
+    for o in range(wide_o // ntz):
+        g_gc[:, o, :] = total[32 * o : 32 * o + 27, :]
+    stores.append(pltpu.make_async_copy(g_gc, o_gc, ws.at[4]))
+    stores[4].start()
     for copy in stores:
         copy.wait()
 

time: 40.9 us -> 39 us (0.954); the launches traced: 40.7 us -> 38.4 us
  Pallas kernels: 40.1 us -> 37.7 us
    pallas_call x1, Pallas kernels: 38 us -> 35.6 us  [per_device(): pl.pallas_call(functools.partial(kernel, sizes), out_shape=(jax.ShapeDtyp...]
where the time goes in v10:
time: 39 us; the launch traced here: 38.4 us
  Pallas kernels  37.7 us (97%)
  between operations  0.64 us (2%)
    pallas_call x1, Pallas kernels, per_device(): pl.pallas_call(functools.partial(kernel, sizes), out_shape=(jax.ShapeDtyp...  35.6 us
    pallas_call x1, Pallas kernels, per_device(): pl.pallas_call(finish, out_shape=(jax.ShapeDtypeStruct((32, 64, 128), BF)...  2.11 us

profile of v10, /device:TPU:1, one launch (start us, length us, event | category | flops | bytes accessed | tf_op | source)
XLA Modules:
  0.0 38.4 jit_solution(16602310924598779234)
XLA Ops:
  0.6 35.6 %shard_map.110 = (bf16[32,64,128]{2,1,0:T(8,128)(2,1)}, f32[16,16,27]{2,1,0:T(8,128)}, f32[16,16,27]{2,1,0:T(8,128)}, bf16[1024,128]{1,0:T(8,128)(2,1)}, f32[27,2,128]{2,1,0:T(2,128)}) custom-call(bf16[32,64,128]{2,1,0:T(8,128)(2,1)} %bitcast.17, bf16[32,64,128]{2,1,0:T(8,128)(2,1)} %bitcast.18, bf16[256,27]{1,0:T(8,128)(2,1)} %bitcast.21, ...), custom_call_target="tpu_custom_call" | custom-call | tf_op jit(solution)/shard_map/pallas_call | solution.py:695
  36.3 2.1 %shard_map.111 = (bf16[32,64,128]{2,1,0:T(8,128)(2,1)}, f32[16,16,27]{2,1,0:T(8,128)}, f32[16,16,27]{2,1,0:T(8,128)}, bf16[1024,128]{1,0:T(8,128)(2,1)}, f32[27,2,128]{2,1,0:T(2,128)}) custom-call(bf16[32,64,128]{2,1,0:T(8,128)(2,1)} %get-tuple-element.15.refs_0_, f32[16,16,27]{2,1,0:T(8,128)} %get-tuple-element.16.refs_1_, ...), custom_call_target="tpu_custom_call" | custom-call | tf_op jit(solution)/shard_map/pallas_call | solution.py:720

commit v11 on v10

--- a/solution.py
+++ b/solution.py
@@ -439,11 +439,12 @@
     core, xme = lax.rem(ty, 2), lax.div(ty, 2)
     other = (dp, ty + 1 - 2 * core, tz)
     hop0 = []
-    g = mm(vmat[...].reshape(1152, 1152), inp3[...], TN)
     for b in range(3):
+        left = vmat[:, :, 384 * b : 384 * b + 384].reshape(1152, 384)
+        g = mm(left, inp3[...], TN)
         for a in range(3):
             for cc in range(3):
-                first = 384 * b + 128 * cc
+                first = 128 * cc
                 part = g[first : first + 128, 128 * a : 128 * a + 128]
                 rsend[9 * b + 3 * a + cc] = part.astype(BF).reshape(nx, 2, wide_o, 128)
         src = rsend.at[pl.ds(9 * b, 9), :, 1 - core]

time: 39 us -> 38.9 us (level)
  the two profiles are of different devices: /device:TPU:1 before, /device:TPU:0 now
where the time goes in v11:
time: 38.9 us; the launch traced here: 38.7 us
  Pallas kernels  38.1 us (98%)
  between operations  0.64 us (2%)
    pallas_call x1, Pallas kernels, per_device(): pl.pallas_call(functools.partial(kernel, sizes), out_shape=(jax.ShapeDtyp...  36 us
    pallas_call x1, Pallas kernels, per_device(): pl.pallas_call(finish, out_shape=(jax.ShapeDtypeStruct((32, 64, 128), BF)...  2.11 us

profile of v11, /device:TPU:0, one launch (start us, length us, event | category | flops | bytes accessed | tf_op | source)
XLA Modules:
  0.0 38.7 jit_solution(8061323056686830193)
XLA Ops:
  0.6 36.0 %shard_map.110 = (bf16[32,64,128]{2,1,0:T(8,128)(2,1)}, f32[16,16,27]{2,1,0:T(8,128)}, f32[16,16,27]{2,1,0:T(8,128)}, bf16[1024,128]{1,0:T(8,128)(2,1)}, f32[27,2,128]{2,1,0:T(2,128)}) custom-call(bf16[32,64,128]{2,1,0:T(8,128)(2,1)} %bitcast.17, bf16[32,64,128]{2,1,0:T(8,128)(2,1)} %bitcast.18, bf16[256,27]{1,0:T(8,128)(2,1)} %bitcast.21, ...), custom_call_target="tpu_custom_call" | custom-call | tf_op jit(solution)/shard_map/pallas_call | solution.py:696
  36.6 2.1 %shard_map.111 = (bf16[32,64,128]{2,1,0:T(8,128)(2,1)}, f32[16,16,27]{2,1,0:T(8,128)}, f32[16,16,27]{2,1,0:T(8,128)}, bf16[1024,128]{1,0:T(8,128)(2,1)}, f32[27,2,128]{2,1,0:T(2,128)}) custom-call(bf16[32,64,128]{2,1,0:T(8,128)(2,1)} %get-tuple-element.15.refs_0_, f32[16,16,27]{2,1,0:T(8,128)} %get-tuple-element.16.refs_1_, ...), custom_call_target="tpu_custom_call" | custom-call | tf_op jit(solution)/shard_map/pallas_call | solution.py:721
